TPU v7x, 512 devices: a whole 4x4x16 slice. The times are simulated.
512 devices in a mesh: dp: 128 (over y, z, core), mp: 4 (over x).
Axes of the slice: x: 4, y: 4, z: 16, core: 2. Of those that a mesh axis runs over, the one named last changes fastest.
Arguments:
- dense_input: bfloat16 [16384, 128], P('dp'), may hold values from -6 to 6
- labels: int32 [16384], P('dp'), may hold values 0 or 1
- table: float32 [32768, 8, 128], P('dp'), may hold values from -4 to 4
- adagrad_state: float32 [32768, 8], P('dp'), may hold values from 1e-05 to 0.001
- new_owner: int32 [32768], P('dp'), may hold values from 0 to 127, as said below
- bag_owner: int32 [49152, 1], P('dp'), may hold values from 0 to 127; in each aligned block of 384 rows (0 to 383, 384 to 767, ...) at most 6 rows name the same one
- bag_slot: int32 [49152], P('dp'), may hold values from 0 to 255
- bag_offsets: int32 [49152, 16], P('dp'), may hold values from 0 to 7
- bag_length: int32 [49152], P('dp'), may hold values from 1 to 16
- w_first: bfloat16 [512, 4096], P(None, 'mp'), may hold values from -0.25 to 0.25
- b_first: float32 [4096], P('mp'), may hold values from -3 to 3
- w_out: float32 [4096], P('mp'), may hold values from -0.09375 to 0.09375
Outputs:
- updated_table: float32 [32768, 8, 128], P('dp')
- updated_state: float32 [32768, 8], P('dp')
- grad_w1: bfloat16 [512, 4096], P(None, 'mp')
- grad_b1: float32 [4096], P('mp')
- grad_w2: float32 [4096], P('mp')
Inputs may be any that keep to these rules, and one draw needn't show every extreme that they name: `new_owner`: every owner receives exactly 256 blocks; a device sends at most 2 blocks to one owner, and exactly 2 to some owner. `bag_owner`: among the bags of one device, at most 6 name one owner.
All inputs are finite; a program needn't handle non-finite values. No bound on the sum of `labels` on one device may be relied on, other than what follows from the above.
Results may differ from a plain program's by a relative error of at most 0.0052.
Values may be sent and summed in bfloat16 or wider, within the bound.
A program may use at most 64 MiB of HBM per device.

v0:
```python
import math

import jax
import jax.numpy as jnp
from jax import lax
from jax.sharding import PartitionSpec as P

learn_rate = 0.01
epsilon = 1e-08


def silu_slope(pre_act):
    sigmoid_val = jax.nn.sigmoid(pre_act)
    return sigmoid_val * (1.0 + pre_act * (1.0 - sigmoid_val))


def ranks_of(target_owner, peer_count):
    onehot = (target_owner[:, None] == jnp.arange(peer_count, dtype=jnp.int32)[None, :]).astype(
        jnp.int32
    )
    running = jnp.cumsum(onehot, axis=0)
    return jnp.sum(running * onehot, axis=1) - 1


def count_rows(index_rows, total_rows):
    lane_ids = jnp.arange(total_rows, dtype=jnp.int32)[None, :]
    counts = jnp.zeros((index_rows.shape[0], total_rows), jnp.float32)
    for lane_pos in range(index_rows.shape[1]):
        counts = counts + (index_rows[:, lane_pos : lane_pos + 1] == lane_ids).astype(jnp.float32)
    return counts


def pool_bags(index_rows, low_table):
    row_count = index_rows.shape[0]
    block_rows = math.gcd(row_count, 512)
    grouped = index_rows.reshape(row_count // block_rows, block_rows, index_rows.shape[1])

    def one_group(bag_group):
        counts = count_rows(bag_group, low_table.shape[0]).astype(jnp.bfloat16)
        return jnp.dot(counts, low_table, preferred_element_type=jnp.float32)

    pooled = lax.map(one_group, grouped)
    return pooled.reshape(row_count, low_table.shape[1])


def row_grads(index_rows, bag_grads, total_rows):
    row_count = index_rows.shape[0]
    block_rows = math.gcd(row_count, 512)
    grouped = index_rows.reshape(row_count // block_rows, block_rows, index_rows.shape[1])
    grad_groups = bag_grads.reshape(row_count // block_rows, block_rows, bag_grads.shape[1])

    def add_group(running_sum, group_pair):
        counts = count_rows(group_pair[0], total_rows)
        term = lax.dot_general(
            counts,
            group_pair[1],
            (((0,), (0,)), ((), ())),
            precision=lax.Precision.HIGHEST,
            preferred_element_type=jnp.float32,
        )
        return (running_sum + term, None)

    start_sum = jnp.zeros((total_rows, bag_grads.shape[1]), jnp.float32)
    result, unused = lax.scan(add_group, start_sum, (grouped, grad_groups))
    return result


def local(
    dense_input,
    labels,
    table,
    adagrad_state,
    new_owner,
    bag_owner,
    bag_slot,
    bag_offsets,
    bag_length,
    w_first,
    b_first,
    w_out,
):
    peer_count = lax.axis_size("dp")
    blocks, rows_blk, emb_width = table.shape
    slot_cap = max(2, -(-blocks // peer_count))
    block_rank = ranks_of(new_owner, peer_count)
    slot_place = new_owner * slot_cap + block_rank
    send_rows = (
        jnp.zeros((peer_count * slot_cap, rows_blk, emb_width), jnp.float32)
        .at[slot_place]
        .set(table)
    )
    send_state = (
        jnp.zeros((peer_count * slot_cap, rows_blk), jnp.float32).at[slot_place].set(adagrad_state)
    )
    got_rows, got_state = (
        lax.all_to_all(
            send_rows.reshape(peer_count, slot_cap, rows_blk, emb_width),
            "dp",
            split_axis=0,
            concat_axis=0,
            tiled=True,
        ),
        lax.all_to_all(
            send_state.reshape(peer_count, slot_cap, rows_blk),
            "dp",
            split_axis=0,
            concat_axis=0,
            tiled=True,
        ),
    )
    got_rows = got_rows.reshape(peer_count * slot_cap, rows_blk, emb_width)
    got_state = got_state.reshape(peer_count * slot_cap, rows_blk)
    filled = (got_state[:, 0] > 0.0).astype(jnp.int32)
    target = jnp.where(filled > 0, jnp.cumsum(filled) - 1, blocks)
    moved_rows = jnp.zeros_like(table).at[target].set(got_rows, mode="drop")
    moved_state = jnp.zeros_like(adagrad_state).at[target].set(got_state, mode="drop")
    bag_count = bag_slot.shape[0]
    bag_cap = max(2, 2 * bag_count // peer_count)
    owners = bag_owner[:, 0]
    bag_rank = ranks_of(owners, peer_count)
    bag_place = owners * bag_cap + bag_rank
    lane_ids = jnp.arange(bag_offsets.shape[1], dtype=jnp.int32)[None, :]
    local_rows = jnp.where(
        lane_ids < bag_length[:, None], bag_slot[:, None] * rows_blk + bag_offsets, -1
    )
    send_index = (
        jnp.full((peer_count * bag_cap, local_rows.shape[1]), -1, jnp.int32)
        .at[bag_place]
        .set(local_rows)
    )
    low_table = moved_rows.reshape(blocks * rows_blk, emb_width).astype(jnp.bfloat16)
    received = lax.all_to_all(
        send_index.reshape(peer_count, bag_cap, local_rows.shape[1]),
        "dp",
        split_axis=0,
        concat_axis=0,
        tiled=True,
    )
    item_count = received.shape[1]
    flat_index = received.reshape(peer_count * item_count, received.shape[2])
    pooled = pool_bags(flat_index, low_table).astype(jnp.bfloat16)
    returned = lax.all_to_all(
        pooled.reshape(peer_count, item_count, emb_width),
        "dp",
        split_axis=0,
        concat_axis=0,
        tiled=True,
    )
    returned, held_index = (returned, received)
    bag_pooled = returned.reshape(peer_count * bag_cap, emb_width)[bag_place]
    samples = dense_input.shape[0]
    features = jnp.concatenate([dense_input, bag_pooled.reshape(samples, -1)], axis=1)
    hidden_pre = jnp.dot(features, w_first, preferred_element_type=jnp.float32) + b_first
    active = jax.nn.silu(hidden_pre)
    part_logit = jnp.dot(active, w_out, precision=lax.Precision.HIGHEST)
    logit_vals = lax.psum(part_logit, "mp")
    logit_grad = jax.nn.sigmoid(logit_vals) - labels.astype(jnp.float32)
    grad_pre = logit_grad[:, None] * w_out[None, :] * silu_slope(hidden_pre)
    grad_low = grad_pre.astype(jnp.bfloat16)
    term_w1 = lax.dot_general(
        features, grad_low, (((0,), (0,)), ((), ())), preferred_element_type=jnp.float32
    )
    term_w2 = jnp.dot(logit_grad, active, precision=lax.Precision.HIGHEST)
    term_b1 = jnp.sum(grad_pre, axis=0)
    part_input = lax.dot_general(
        grad_low, w_first[emb_width:], (((1,), (1,)), ((), ())), preferred_element_type=jnp.float32
    )
    bag_grad = (
        lax.psum(part_input.astype(jnp.bfloat16), "mp")
        .astype(jnp.float32)
        .reshape(bag_count, emb_width)
    )
    send_grad = (
        jnp.zeros((peer_count * bag_cap, emb_width), jnp.float32).at[bag_place].set(bag_grad)
    )
    owner_grad = lax.all_to_all(
        send_grad.reshape(peer_count, bag_cap, emb_width).astype(jnp.bfloat16),
        "dp",
        split_axis=0,
        concat_axis=0,
        tiled=True,
    ).astype(jnp.float32)
    grad_rows = row_grads(
        held_index.reshape(peer_count * bag_cap, -1),
        owner_grad.reshape(peer_count * bag_cap, emb_width),
        blocks * rows_blk,
    )
    grad_rows = grad_rows.reshape(blocks, rows_blk, emb_width)
    updated_state = moved_state + jnp.mean(grad_rows * grad_rows, axis=2)
    updated_table = moved_rows - learn_rate * grad_rows / (
        jnp.sqrt(updated_state)[:, :, None] + epsilon
    )
    sum_w1, sum_w2, sum_b1 = lax.psum((term_w1, term_w2, term_b1), "dp")
    grad_first = sum_w1.astype(jnp.bfloat16)
    return (updated_table, updated_state, grad_first, sum_b1, sum_w2)


def solution(mesh):
    placed = (
        P("dp", None),
        P("dp"),
        P("dp", None, None),
        P("dp", None),
        P("dp"),
        P("dp", None),
        P("dp"),
        P("dp", None),
        P("dp"),
        P(None, "mp"),
        P("mp"),
        P("mp"),
    )
    return jax.shard_map(
        local,
        mesh=mesh,
        in_specs=placed,
        out_specs=(P("dp", None, None), P("dp", None), P(None, "mp"), P("mp"), P("mp")),
        check_vma=False,
    )
```

profile of v0, /device:TPU:1, one launch (start us, length us, event | category | flops | bytes accessed | tf_op | source)
XLA Modules:
  0.0 842.6 jit_solution(9691115527239635056)
XLA Ops:
  12.4 20.6 %all-to-all-start = ((f32[128,2,8]{2,1,0:T(2,128)}), f32[128,2,8]{2,1,0:T(2,128)S(1)}, u32[]{:S(2)}, u32[]{:S(2)}) async-start(f32[128,2,8]{2,1,0:T(2,128)} %bitcast.22), calls=%async_computation | async-start | bytes 262144 | tf_op jit(solution)/shard_map/all_to_all | solution.py:103
  37.7 12.7 %all-to-all-done = f32[128,2,8]{2,1,0:T(2,128)S(1)} async-done(((f32[128,2,8]{2,1,0:T(2,128)}), f32[128,2,8]{2,1,0:T(2,128)S(1)}, u32[]{:S(2)}, u32[]{:S(2)}) %all-to-all-start) | async-done | bytes 8224 | tf_op jit(solution)/shard_map/all_to_all | solution.py:103
  50.4 6.9 all-to-all-start.2
  58.4 25.5 %scatter_fusion = f32[256,8,128]{2,1,0:T(8,128)} fusion(f32[256,8,128]{2,1,0:T(8,128)} %broadcast.113.clone, s32[256]{0:T(256)S(1)} %compare_select_fusion.2, f32[256,8,128]{2,1,0:T(8,128)S(1)} %copy-done), kind=kCustom, calls=%fused_computation.2 | custom fusion | bytes 3146752 | tf_op jit(solution)/shard_map/scatter | solution.py:90
  83.9 6.8 all-to-all-done.2
  90.7 9.5 %all-to-all-start.1 = ((f32[128,2,8,128]{3,2,1,0:T(8,128)}), f32[128,2,8,128]{3,2,1,0:T(8,128)S(1)}, u32[]{:S(2)}, u32[]{:S(2)}) async-start(f32[128,2,8,128]{3,2,1,0:T(8,128)} %bitcast.25), calls=%async_computation.1 | async-start | bytes 2097152 | tf_op jit(solution)/shard_map/all_to_all | solution.py:96
  101.4 53.2 %all-to-all-done.1 = f32[128,2,8,128]{3,2,1,0:T(8,128)S(1)} async-done(((f32[128,2,8,128]{3,2,1,0:T(8,128)}), f32[128,2,8,128]{3,2,1,0:T(8,128)S(1)}, u32[]{:S(2)}, u32[]{:S(2)}) %all-to-all-start.1) | async-done | bytes 1048608 | tf_op jit(solution)/shard_map/all_to_all | solution.py:96
  154.7 7.0 scatter_fusion.1
  161.8 15.4 %while.21 = (s32[]{:T(128)}, bf16[3,256,128]{2,1,0:T(8,128)(2,1)S(1)}, s32[3,256,16]{1,2,0:T(8,128)S(1)}, bf16[2048,128]{1,0:T(8,128)(2,1)S(1)}, s32[]{:T(128)}) while((s32[]{:T(128)}, bf16[3,256,128]{2,1,0:T(8,128)(2,1)S(1)}, s32[3,256,16]{1,2,0:T(8,128)S(1)}, bf16[2048,128]{1,0:T(8,128)(2,1)S(1)}, s32[]{:T(128)}) %tuple.81), condition=%wide.region_13.14_spmd, body=%wide.region_12.13_spmd.sunk | while | flops 159383552 | bytes 737357 | solution.py:42
  161.8 5.1 fusion.113
  167.0 5.1 fusion.113
  172.1 5.1 fusion.113
  178.0 8.8 %all-to-all-start.3 = ((bf16[128,6,128]{2,1,0:T(8,128)(2,1)}), bf16[128,6,128]{2,1,0:T(8,128)(2,1)S(1)}, u32[]{:S(2)}, u32[]{:S(2)}) async-start(bf16[128,6,128]{2,1,0:T(8,128)(2,1)} %convert_element_type.160), calls=%async_computation.3 | async-start | bytes 524288 | tf_op jit(solution)/shard_map/all_to_all | solution.py:142
  188.1 21.2 %all-to-all-done.3 = bf16[128,6,128]{2,1,0:T(8,128)(2,1)S(1)} async-done(((bf16[128,6,128]{2,1,0:T(8,128)(2,1)}), bf16[128,6,128]{2,1,0:T(8,128)(2,1)S(1)}, u32[]{:S(2)}, u32[]{:S(2)}) %all-to-all-start.3) | async-done | bytes 196640 | tf_op jit(solution)/shard_map/all_to_all | solution.py:142
  213.1 8.5 %psum.35 = f32[128]{0:T(128)S(1)} all-reduce(f32[128]{0:T(128)S(1)} %convolution_bitcast_fusion.1), channel_id=1, replica_groups=mesh['dp'=128,'mp'=4] {'mp'}, use_global_device_ids=true, to_apply=%region_14.15 | all-reduce | flops 128 | bytes 1024 | tf_op jit(solution)/shard_map/psum | solution.py:156
  223.2 1.9 fusion.80
  226.0 45.5 %all-reduce.4.cloned.1.call-done = bf16[384,128]{1,0:T(8,128)(2,1)} async-done(((bf16[384,128]{1,0:T(8,128)(2,1)}), bf16[384,128]{1,0:T(8,128)(2,1)}) %all-reduce.4.cloned.1.call-update) | async-done | bytes 98320 | tf_op jit(solution)/shard_map/psum | solution.py:169
  271.5 1.9 scatter_custom_fusion.4
  274.2 18.7 %all-to-all-start.4 = ((bf16[128,6,128]{2,1,0:T(8,128)(2,1)}), bf16[128,6,128]{2,1,0:T(8,128)(2,1)S(1)}, u32[]{:S(2)}, u32[]{:S(2)}) async-start(bf16[128,6,128]{2,1,0:T(8,128)(2,1)} %convert_element_type.165), calls=%async_computation.4 | async-start | bytes 524288 | tf_op jit(solution)/shard_map/all_to_all | solution.py:176
  292.9 517.0 %all-reduce.5 = (bf16[512,1024]{1,0:T(8,128)(2,1)}, f32[1024]{0:T(1024)}, f32[1024]{0:T(1024)}) all-reduce(f32[512,1024]{1,0:T(8,128)} %fusion.80, f32[1024]{0:T(1024)S(1)} %fusion.97, f32[1024]{0:T(1024)S(1)} %bitcast.211), channel_id=1, replica_groups=mesh['dp'=128,'mp'=4] {'dp'}, use_global_device_ids=true, to_apply=%region_21.22 | all-reduce | flops 526336 | bytes 3162112 | tf_op jit(solution)/shard_map/psum | solution.py:193
  810.0 23.2 %while.22 = (s32[]{:T(128)}, f32[2048,128]{1,0:T(8,128)S(1)}, s32[3,256,16]{1,2,0:T(8,128)S(1)}, f32[3,256,128]{2,1,0:T(8,128)S(1)}, s32[]{:T(128)}, /*index=5*/s32[]{:T(128)}) while((s32[]{:T(128)}, f32[2048,128]{1,0:T(8,128)S(1)}, s32[3,256,16]{1,2,0:T(8,128)S(1)}, f32[3,256,128]{2,1,0:T(8,128)S(1)}, s32[]{:T(128)}, ...), condition=%wide.region_18.19_spmd.clone, body=%wide.region_17.18_spmd.clone.sunk | while | flops 830472192 | bytes 2310239 | solution.py:64
  810.1 7.7 convolution_add_fusion.3
  817.8 7.7 convolution_add_fusion.3
  825.5 7.7 convolution_add_fusion.3
  (99 shorter events, 23.9 us)
Async XLA Ops:
  7.2 28.0 %copy-start.4 = (s32[384,1]{0,1:T(1,128)S(1)}, s32[384,1]{0,1:T(1,128)}, u32[]{:S(2)}) copy-start(s32[384,1]{0,1:T(1,128)} %param.21) | copy-start | bytes 4612
  7.2 27.9 %copy-start.7 = (s32[384]{0:T(512)S(1)}, s32[384]{0:T(512)}, u32[]{:S(2)}) copy-start(s32[384]{0:T(512)} %param.24) | copy-start | bytes 4612
  7.2 27.9 %copy-start.3 = (s32[384,16]{0,1:T(8,128)S(1)}, s32[384,16]{0,1:T(8,128)}, u32[]{:S(2)}) copy-start(s32[384,16]{0,1:T(8,128)} %param.23) | copy-start | bytes 73732
  12.4 38.0 %all-to-all-start = ((f32[128,2,8]{2,1,0:T(2,128)}), f32[128,2,8]{2,1,0:T(2,128)S(1)}, u32[]{:S(2)}, u32[]{:S(2)}) async-start(f32[128,2,8]{2,1,0:T(2,128)} %bitcast.22), calls=%async_computation | async-start | bytes 262144 | tf_op jit(solution)/shard_map/all_to_all | solution.py:103
  34.8 23.6 %copy-start = (f32[256,8,128]{2,1,0:T(8,128)S(1)}, f32[256,8,128]{2,1,0:T(8,128)}, u32[]{:S(2)}) copy-start(f32[256,8,128]{2,1,0:T(8,128)} %param.18) | copy-start | bytes 3145732
  50.4 40.3 %all-to-all-start.2 = ((s32[128,6,16]{2,1,0:T(8,128)}), s32[128,6,16]{2,1,0:T(8,128)S(1)}, u32[]{:S(2)}, u32[]{:S(2)}) async-start(s32[128,6,16]{2,1,0:T(8,128)} %reshape.147), calls=%async_computation.2 | async-start | bytes 1048576 | tf_op jit(solution)/shard_map/all_to_all | solution.py:132
  90.7 63.9 %all-to-all-start.1 = ((f32[128,2,8,128]{3,2,1,0:T(8,128)}), f32[128,2,8,128]{3,2,1,0:T(8,128)S(1)}, u32[]{:S(2)}, u32[]{:S(2)}) async-start(f32[128,2,8,128]{3,2,1,0:T(8,128)} %bitcast.25), calls=%async_computation.1 | async-start | bytes 2097152 | tf_op jit(solution)/shard_map/all_to_all | solution.py:96
  161.7 25.1 %copy-start.2 = (bf16[128,128]{1,0:T(8,128)(2,1)S(1)}, bf16[128,128]{1,0:T(8,128)(2,1)}, u32[]{:S(2)}) copy-start(bf16[128,128]{1,0:T(8,128)(2,1)} %param.16) | copy-start | bytes 98308
  177.2 33.7 %copy-start.5 = (f32[1024]{0:T(1024)S(1)}, f32[1024]{0:T(1024)}, u32[]{:S(2)}) copy-start(f32[1024]{0:T(1024)} %param.26) | copy-start | bytes 12292
  178.0 34.5 %copy-start.6 = (f32[1024]{0:T(1024)S(1)}, f32[1024]{0:T(1024)}, u32[]{:S(2)}) copy-start(f32[1024]{0:T(1024)} %param.27) | copy-start | bytes 12292
  178.0 31.3 %all-to-all-start.3 = ((bf16[128,6,128]{2,1,0:T(8,128)(2,1)}), bf16[128,6,128]{2,1,0:T(8,128)(2,1)S(1)}, u32[]{:S(2)}, u32[]{:S(2)}) async-start(bf16[128,6,128]{2,1,0:T(8,128)(2,1)} %convert_element_type.160), calls=%async_computation.3 | async-start | bytes 524288 | tf_op jit(solution)/shard_map/all_to_all | solution.py:142
  186.8 84.8 %all-reduce.4.cloned.1.call-start = ((), (), s32[]{:S(2)}) async-start(), calls=%async_computation.5 | async-start | bytes 196608 | tf_op jit(solution)/shard_map/psum | solution.py:169
  210.9 10.7 %copy-start.8 = (s32[128]{0:T(128)S(1)}, s32[128]{0:T(128)}, u32[]{:S(2)}) copy-start(s32[128]{0:T(128)} %param.17) | copy-start | bytes 1540
  221.5 1.2 copy-start.1
  274.2 535.7 %all-to-all-start.4 = ((bf16[128,6,128]{2,1,0:T(8,128)(2,1)}), bf16[128,6,128]{2,1,0:T(8,128)(2,1)S(1)}, u32[]{:S(2)}, u32[]{:S(2)}) async-start(bf16[128,6,128]{2,1,0:T(8,128)(2,1)} %convert_element_type.165), calls=%async_computation.4 | async-start | bytes 524288 | tf_op jit(solution)/shard_map/all_to_all | solution.py:176
Sparse Core Ops, SparseCore 0:
  225.9 45.5 all-reduce.3
where the time goes:
time: 847 us; the launch traced here: 843 us
  blocking collectives  525 us (62%)
  waiting for transfers between devices  139 us (16%)
  starting transfers between devices  64.5 us (8%)
  local copies, waits for them, and re-layouts  47 us (6%)
  matrix products  43.2 us (5%)
  between operations  14.5 us (2%)
    psum x1, blocking collectives, local(): sum_w1, sum_w2, sum_b1 = lax.psum((term_w1, term_w2, term_b1), 'dp')  517 us
    all_to_all x1, waiting for transfers between devices, local(): lax.all_to_all(send_rows.reshape(peer_count, slot_cap, rows_blk, emb_widt...  53.2 us
    psum x1, waiting for transfers between devices, local(): lax.psum(part_input.astype(jnp.bfloat16), 'mp').astype(jnp.float32)  45.5 us
    scatter x1, local copies, waits for them, and re-layouts, local(): send_rows = jnp.zeros((peer_count * slot_cap, rows_blk, emb_width), jnp.f...  25.5 us
    dot_general x3, matrix products, add_group(): lax.dot_general(counts, group_pair[1], (((0,), (0,)), ((), ())), precisio...  23 us
    all_to_all x1, waiting for transfers between devices, local(): lax.all_to_all(pooled.reshape(peer_count, item_count, emb_width), 'dp', s...  21.2 us
    all_to_all x1, starting transfers between devices, local(): lax.all_to_all(send_state.reshape(peer_count, slot_cap, rows_blk), 'dp',...  20.6 us
    all_to_all x1, starting transfers between devices, local(): lax.all_to_all(send_grad.reshape(peer_count, bag_cap, emb_width).astype(j...  18.7 us
  transfers between devices with their start and end apart: 6, of which 5 were waited for; matrix products, arithmetic and copies ran while one was open for 4% of the time, Pallas kernels for 0%

commit v1 on v0

v1 whole, which is shorter than its diff:
```python
import functools

import jax
import jax.numpy as jnp
from jax import lax
from jax.experimental import pallas as pl
from jax.experimental.pallas import tpu as pltpu
from jax.sharding import PartitionSpec as P

MESH = pl.DeviceIdType.MESH
BF = jnp.bfloat16
F32 = jnp.float32
I32 = jnp.int32
learn_rate = 0.01
epsilon = 1e-08
W = 128


def iota(shape, dim):
    return lax.broadcasted_iota(I32, shape, dim)


def dot(a, b, dims=((1,), (0,)), exact=False):
    return lax.dot_general(
        a,
        b,
        (dims, ((), ())),
        precision=lax.Precision.HIGHEST if exact else None,
        preferred_element_type=F32,
    )


def log2(n):
    return n.bit_length() - 1


def onehot(mask):
    return jnp.where(mask, 1.0, 0.0).astype(BF)


def to_col(row, rows, pick):
    return jnp.sum(jnp.where(pick, row, 0.0), axis=1, keepdims=True)


class Shape:
    def __init__(self, dp, mp, blocks, samples, hidden):
        self.C = 2
        self.Y = 4 if dp == 128 else 2
        self.Z = dp // (self.C * self.Y)
        self.M = mp
        self.K = self.Z // mp
        self.G = self.Y * self.C
        self.N = dp
        self.NB = blocks
        self.B = samples
        self.HL = hidden
        self.T = self.G * self.K
        self.RY = 512 // (self.C * self.Y)
        self.RG = min(self.Z, self.RY // 16)
        self.CG = self.Z // self.RG
        self.pr = self.RY // self.RG
        self.pc = hidden // self.CG
        self.V = hidden // (W * self.Y)


def kernel(
    S,
    owner_ref,
    bown_ref,
    bslot_ref,
    boff_ref,
    blen_ref,
    dense_ref,
    label_ref,
    table_ref,
    state_ref,
    w_ref,
    b_ref,
    wo_ref,
    out_t,
    out_s,
    out_w,
    out_v,
    stage_t,
    send_t,
    send_r,
    mid_t,
    mid_r,
    recv_t,
    recv_r,
    rmat,
    pooled,
    mid_p,
    send_p,
    slots,
    lbuf,
    act,
    slope,
    feat,
    part_s,
    recv_x,
    send_g,
    mid_g,
    send_h,
    recv_g,
    send_c,
    keep_c,
    recv_c,
    send_y,
    keep_y,
    recv_y,
    send_z,
    recv_z,
    vec,
    vec_c,
    vec_y,
    vec_ys,
    vec_z,
    ss,
    rs,
    sr,
    rr,
):
    C, Y, Z, M, K, G, N, NB, B, HL, T = S.C, S.Y, S.Z, S.M, S.K, S.G, S.N, S.NB, S.B, S.HL, S.T
    B3 = 3 * B
    NS = N * 8
    lY, lZ, lM, lK, lG = log2(Y), log2(Z), log2(M), log2(K), log2(G)
    me = lax.axis_index("dp")
    m = lax.axis_index("mp")
    c = lax.rem(me, C)
    z = lax.rem(me // C, Z)
    y = me // (C * Z)
    g = y * C + c
    half = M // 2
    home = lax.rem(z + half * c, M)
    conc = home == m
    base_z = lax.rem(m + M - half * c, M)

    def dp_of(gg, zz):
        return ((gg // C) * Z + zz) * C + lax.rem(gg, C)

    def remote(src, dst, i, dp, mp, small=False):
        pltpu.make_async_remote_copy(
            src_ref=src,
            dst_ref=dst,
            send_sem=(sr if small else ss).at[i],
            recv_sem=(rr if small else rs).at[i],
            device_id=(dp, mp),
            device_id_type=MESH,
        ).start()

    def local(src, dst, i, small=False):
        pltpu.make_async_copy(src, dst, (rr if small else rs).at[i]).start()

    def wait_in(ref, i, small=False):
        pltpu.make_async_copy(ref, ref, (rr if small else rs).at[i]).wait()

    def wait_out(ref, i, small=False):
        pltpu.make_async_copy(ref, ref, (sr if small else ss).at[i]).wait()

    def each(lo, hi, body):
        def step(t, carry):
            body(t)
            return carry

        lax.fori_loop(lo, hi, step, 0)

    barrier = pltpu.get_barrier_semaphore()

    def greet(dp, mp):
        pl.semaphore_signal(barrier, inc=1, device_id=(dp, mp), device_id_type=MESH)

    each(1, G, lambda t: greet(dp_of(lax.rem(g + t, G), z), m))
    each(1, Z, lambda t: greet(dp_of(g, lax.rem(z + t, Z)), m))
    each(1, M, lambda t: greet(me, lax.rem(m + t, M)))

    def target_of(tt):
        gg = lax.shift_right_logical(tt, lK)
        kk = tt & (K - 1)
        yy = lax.shift_right_logical(gg, 1)
        cc = gg & 1
        zz = ((m + M - half * cc) & (M - 1)) + M * kk
        return (yy * Z + zz) * C + cc

    own_row = owner_ref[...].astype(F32)
    own_col = to_col(own_row, NB, iota((NB, NB), 0) == iota((NB, NB), 1))
    rank_row = jnp.sum(
        jnp.where((own_col == own_row) & (iota((NB, NB), 0) < iota((NB, NB), 1)), 1.0, 0.0),
        axis=0,
        keepdims=True,
    )
    rows2 = iota((2 * T, 1), 0)
    want = target_of(lax.shift_right_logical(rows2, 1)).astype(F32)
    pick_f = jnp.where((own_row == want) & (rank_row == (rows2 & 1).astype(F32)), 1.0, 0.0)
    pick = pick_f.astype(BF)
    for r in range(8):
        low = table_ref[pl.ds(r, NB, stride=8), :].astype(BF)
        stage_t[pl.ds(r, 2 * T, stride=8), :] = dot(pick, low)
    send_t[...] = stage_t[...].astype(BF).reshape(G, K, 16, W)

    bo_row = bown_ref[...].astype(F32)
    eye = iota((B3, B3), 0) == iota((B3, B3), 1)
    bo_col = to_col(bo_row, B3, eye)
    same = bo_col == bo_row
    brank_col = jnp.sum(jnp.where(same & (iota((B3, B3), 1) < iota((B3, B3), 0)), 1.0, 0.0), axis=1, keepdims=True)
    brank_row = jnp.sum(jnp.where(same & (iota((B3, B3), 0) < iota((B3, B3), 1)), 1.0, 0.0), axis=0, keepdims=True)
    slot_nat = bslot_ref[...]
    sy = lax.shift_right_logical(slot_nat, lZ + 2)
    sz = lax.shift_right_logical(slot_nat, 2) & (Z - 1)
    slot_z = ((sz * Y + sy) * 4 + (slot_nat & 3)).astype(F32)
    slot_col = to_col(slot_z, B3, eye)
    len_col = to_col(blen_ref[...].astype(F32), B3, eye)
    lane = iota((B3, W), 1)
    spread = onehot((iota((16, W), 1) & 15) == iota((16, W), 0))
    off_t = dot(boff_ref[...].astype(F32).astype(BF), spread)
    hit = onehot((off_t == lax.shift_right_logical(lane, 4).astype(F32)) & ((lane & 15).astype(F32) < len_col))
    gather8 = onehot((iota((W, W), 1) & 15) == lax.shift_right_logical(iota((W, W), 0), 4))
    counts = dot(hit, gather8)
    req = jnp.where((lane & 15) == 8, slot_col, counts)
    req = jnp.where(lax.shift_right_logical(lane, 4).astype(F32) == brank_col, req, 0.0).astype(BF)
    want_t = target_of(iota((T, 1), 0)).astype(F32)
    rows = dot(onehot(bo_row == want_t), req)
    for p in range(2):
        put = jnp.where(iota((8, W), 1) == iota((8, W), 0) + 96 + 8 * p, 1.0, 0.0)
        placed = dot(state_ref[...], put, exact=True)
        pick_p = jnp.where((own_row == want_t) & (rank_row == float(p)), 1.0, 0.0)
        rows = rows + dot(pick_p, placed, exact=True)
    for t in range(T):
        send_r[t // K, t % K] = rows[t : t + 1, :]

    pl.semaphore_wait(barrier, (G - 1) + (Z - 1) + (M - 1))

    local(send_r.at[g], mid_r.at[g], 0, True)
    local(send_t.at[g], mid_t.at[g], 0)

    def fwd_a(t):
        gg = lax.rem(g + t, G)
        remote(send_r.at[gg], mid_r.at[g], 0, dp_of(gg, z), m, True)
        remote(send_t.at[gg], mid_t.at[g], 0, dp_of(gg, z), m)

    each(1, G, fwd_a)
    wait_in(mid_r, 0, True)
    wait_in(mid_t, 0)

    def fwd_b(k):
        zz = base_z + M * k

        @pl.when(zz != z)
        def _():
            remote(mid_r.at[:, k], recv_r.at[z], 1, dp_of(g, zz), m, True)
            remote(mid_t.at[:, k], recv_t.at[z], 1, dp_of(g, zz), m)

        @pl.when(zz == z)
        def _():
            local(mid_r.at[:, k], recv_r.at[z], 1, True)
            local(mid_t.at[:, k], recv_t.at[z], 1)

    each(0, K, fwd_b)

    bo = bown_ref[...]
    oc = bo & 1
    oz = lax.shift_right_logical(bo, 1) & (Z - 1)
    oy = lax.shift_right_logical(bo, 1 + lZ)
    om = (oz + half * oc) & (M - 1)
    ok = lax.shift_right_logical(oz, lM)
    place = (((om * G + oy * C + oc) * K + ok) * 8).astype(F32) + brank_row
    pcol, prow = [], []
    for f in range(3):
        col = to_col(place, B, iota((B, B3), 1) == 3 * iota((B, B3), 0) + f)
        pcol.append(col)
        prow.append(jnp.sum(jnp.where(iota((B, B), 0) == iota((B, B), 1), col, 0.0), axis=0, keepdims=True))

    pick16 = lax.shift_right_logical(iota((W, W), 0), 4)
    low16 = iota((W, W), 0) & 15
    tile_c = onehot(low16 == (iota((W, W), 1) & 7))
    tile_s = onehot(low16 == 8)
    del pick16

    def flat_rows():
        def one(i):
            rmat[pl.ds(i, 1), :] = recv_r[i // G, lax.rem(i, G)]

        each(0, N, one)

    CH = min(NS, 2 * G * 8)

    def entries(i, n):
        row = iota((n, N), 0) + i * n
        src = onehot(lax.shift_right_logical(row, 3) == iota((n, N), 1))
        wide = dot(src, jnp.where(iota((N, W), 1) < 96, rmat[...], 0.0).astype(BF))
        keep = lax.shift_right_logical(iota((n, W), 1), 4) == (iota((n, W), 0) & 7)
        return jnp.where(keep, wide, 0.0).astype(BF)

    @pl.when(conc)
    def _():
        wait_in(recv_r, 1, True)
        wait_in(recv_t, 1)

        def cast(t):
            remote(recv_r, recv_r, 2, me, lax.rem(m + t, M), True)
            remote(recv_t, recv_t, 2, me, lax.rem(m + t, M))

        each(1, M, cast)
        flat_rows()

        def pool(i):
            ent = entries(i, CH)
            cnt = dot(ent, tile_c)
            slt = dot(ent, tile_s)
            group = lax.shift_right_logical(iota((CH, W), 1), 3)
            parts = [
                jnp.where(slt == (group + 16 * q).astype(F32), cnt, 0.0).astype(BF) for q in range(NB // 16)
            ]
            wide = jnp.concatenate(parts, axis=1) if len(parts) > 1 else parts[0]
            got = dot(wide, recv_t[...].reshape(NB * 8, W))
            per = CH // (G * 8)
            pooled[pl.ds(i * per, per)] = got.astype(BF).reshape(per, G * 8, W)

            def send(q):
                zz = i * per + q

                @pl.when(zz != z)
                def _():
                    remote(pooled.at[zz], mid_p.at[z // M], 3, dp_of(g, zz), m)

                @pl.when(zz == z)
                def _():
                    local(pooled.at[zz], mid_p.at[z // M], 3)

            each(0, per, send)

        each(0, NS // CH, pool)

    wait_in(mid_p, 3)
    R2 = K * G * 8
    ro = iota((R2, R2), 0)
    ri = iota((R2, R2), 1)
    swap = (
        (lax.shift_right_logical(ro, lK + 3) == (lax.shift_right_logical(ri, 3) & (G - 1)))
        & ((lax.shift_right_logical(ro, 3) & (K - 1)) == lax.shift_right_logical(ri, lG + 3))
        & ((ro & 7) == (ri & 7))
    )
    send_p[...] = dot(onehot(swap), mid_p[...].reshape(R2, W)).astype(BF).reshape(G, K * 8, W)
    local(send_p.at[g], slots.at[m, g], 4)

    def ret_a(t):
        gg = lax.rem(g + t, G)
        remote(send_p.at[gg], slots.at[m, g], 4, dp_of(gg, z), m)

    each(1, G, ret_a)
    wait_in(slots.at[m], 4)
    each(1, M, lambda t: remote(slots.at[m], slots.at[m], 5, me, lax.rem(m + t, M)))
    wait_in(slots.at[pl.ds(0, M - 1)], 5)

    table_s = slots[...].reshape(NS, W)
    feat[0] = dense_ref[...]
    for f in range(3):
        feat[f + 1] = dot(onehot(iota((B, NS), 1).astype(F32) == pcol[f]), table_s).astype(BF)
    features = jnp.concatenate([feat[i] for i in range(4)], axis=1)
    pre = dot(features, w_ref[...]) + b_ref[...]
    sig = jax.nn.sigmoid(pre)
    active = pre * sig
    act[...] = active
    slope[...] = sig * (1.0 + pre * (1.0 - sig)) * wo_ref[...]
    part = jnp.sum(active * wo_ref[...], axis=1, keepdims=True)
    eye_b = iota((B, B), 0) == iota((B, B), 1)
    part_row = jnp.sum(jnp.where(eye_b, part, 0.0), axis=0, keepdims=True)
    lbuf[m] = jnp.broadcast_to(part_row, (8, B))
    each(1, M, lambda t: remote(lbuf.at[m], lbuf.at[m], 3, me, lax.rem(m + t, M), True))
    wait_in(lbuf.at[pl.ds(0, M - 1)], 3, True)

    total = lbuf[0]
    for i in range(1, M):
        total = total + lbuf[i]
    lgrad_row = jax.nn.sigmoid(total[0:1, :]) - label_ref[...].astype(F32)
    lgrad = to_col(lgrad_row, B, eye_b)
    grad_pre = lgrad * slope[...]
    grad_low = grad_pre.astype(BF)
    b1 = jnp.sum(grad_pre, axis=0, keepdims=True)
    w2 = jnp.sum(lgrad * act[...], axis=0, keepdims=True)
    for i, row in enumerate((b1, w2)):
        for j in range(HL // W):
            vec[i, j // S.V, pl.ds(j % S.V, 1), :] = row[:, j * W : (j + 1) * W]

    hrows = 512 // C
    other = 1 - c
    mate = me + 1 - 2 * c

    def term_of(i, blk):
        return dot(feat[i], blk, ((0,), (0,)))

    for h in range(C):

        @pl.when(c != h)
        def _():
            for i in range(2):
                send_c[pl.ds(i * W, W), :] = term_of(2 * h + i, grad_low).astype(BF)

        @pl.when(c == h)
        def _():
            for i in range(2):
                keep_c[pl.ds(i * W, W), :] = term_of(2 * h + i, grad_low)

    remote(send_c, recv_c, 6, mate, m)
    remote(vec.at[other], vec_c, 6, mate, m, True)

    inputs = [
        dot(grad_low, w_ref[pl.ds((f + 1) * W, W), :], ((1,), (1,))).astype(BF) for f in range(3)
    ]
    for q in range(M):
        acc = None
        for f in range(3):
            rowid = (iota((R2, B), 0) + q * R2).astype(F32)
            term = dot(onehot(rowid == prow[f]), inputs[f])
            acc = term if acc is None else acc + term
        part_s[q] = acc.astype(BF)

    def xrs(t):
        mm = lax.rem(m + t, M)
        remote(part_s.at[mm], recv_x.at[m], 7, me, mm)

    local(part_s.at[m], recv_x.at[m], 7)
    each(1, M, xrs)

    wait_in(recv_c, 6)
    wait_in(vec_c, 6, True)
    keep_y[...] = keep_c[...] + recv_c[...].astype(F32)
    send_y[...] = keep_y[...].astype(BF).reshape(Y, S.RY, HL)
    vec[c] = vec[c] + vec_c[...]

    def to_y(t):
        yy = lax.rem(y + t, Y)
        remote(send_y.at[yy], recv_y.at[y], 8, (yy * Z + z) * C + c, m)
        remote(vec.at[c, yy], vec_y.at[y], 8, (yy * Z + z) * C + c, m, True)

    each(1, Y, to_y)

    wait_in(recv_x, 7)
    acc = recv_x[0].astype(F32)
    for i in range(1, M):
        acc = acc + recv_x[i].astype(F32)
    send_g[...] = acc.astype(BF).reshape(G, K * 8, W)
    local(send_g.at[g], mid_g.at[g], 9)

    def grad_a(t):
        gg = lax.rem(g + t, G)
        remote(send_g.at[gg], mid_g.at[g], 9, dp_of(gg, z), m)

    each(1, G, grad_a)

    wait_in(recv_y.at[pl.ds(0, Y - 1)], 8)
    wait_in(vec_y.at[pl.ds(0, Y - 1)], 8, True)
    acc = keep_y[pl.ds(pl.multiple_of(y * S.RY, S.RY), S.RY), :]
    accv = vec[c, y]
    for t in range(1, Y):
        yy = lax.rem(y + t, Y)
        acc = acc + recv_y[yy].astype(F32)
        accv = accv + vec_y[yy]
    for i in range(Z):
        r0, c0 = (i // S.CG) * S.pr, (i % S.CG) * S.pc
        send_z[i] = acc[r0 : r0 + S.pr, c0 : c0 + S.pc].astype(BF)
    vec_ys[...] = accv
    local(send_z.at[z], recv_z.at[z], 10)
    local(vec_ys, vec_z.at[z], 10, True)

    def to_z(t):
        zz = lax.rem(z + t, Z)
        remote(send_z.at[zz], recv_z.at[z], 10, dp_of(g, zz), m)
        remote(vec_ys, vec_z.at[z], 10, dp_of(g, zz), m, True)

    each(1, Z, to_z)

    wait_in(mid_g, 9)
    unswap = (
        (lax.shift_right_logical(ri, lK + 3) == (lax.shift_right_logical(ro, 3) & (G - 1)))
        & ((lax.shift_right_logical(ri, 3) & (K - 1)) == lax.shift_right_logical(ro, lG + 3))
        & ((ro & 7) == (ri & 7))
    )
    send_h[...] = dot(onehot(unswap), mid_g[...].reshape(R2, W)).astype(BF).reshape(K, G * 8, W)

    def grad_b(k):
        zz = base_z + M * k

        @pl.when(zz != z)
        def _():
            remote(send_h.at[k], recv_g.at[z], 11, dp_of(g, zz), m)

        @pl.when(zz == z)
        def _():
            local(send_h.at[k], recv_g.at[z], 11)

    each(0, K, grad_b)

    wait_in(recv_z, 10)
    wait_in(vec_z, 10, True)

    def add_z(i, carry):
        return carry[0] + recv_z[i].astype(F32), carry[1] + vec_z[i]

    acc, accv = lax.fori_loop(
        0, Z, add_z, (jnp.zeros((S.pr, S.pc), F32), jnp.zeros((S.V, W), F32))
    )
    block0 = c * hrows + y * S.RY

    def piece(yy, zz):
        r0 = pl.multiple_of(c * hrows + yy * S.RY + (zz // S.CG) * S.pr, 16)
        c0 = pl.multiple_of(lax.rem(zz, S.CG) * S.pc, W)
        return out_w.at[pl.ds(r0, S.pr), pl.ds(c0, S.pc)]

    out_w[
        pl.ds(pl.multiple_of(block0 + (z // S.CG) * S.pr, 16), S.pr),
        pl.ds(pl.multiple_of(lax.rem(z, S.CG) * S.pc, W), S.pc),
    ] = acc.astype(BF)
    out_v[c, y] = accv
    each(1, Z, lambda t: remote(piece(y, z), piece(y, z), 12, dp_of(g, lax.rem(z + t, Z)), m))

    @pl.when(conc)
    def _():
        wait_in(recv_g, 11)
        each(1, M, lambda t: remote(recv_g, recv_g, 13, me, lax.rem(m + t, M)))

    wait_in(send_z.at[pl.ds(0, Z - 1)], 12)
    mine = out_w.at[pl.ds(pl.multiple_of(block0, 16), S.RY), :]

    def ag_y(t):
        yy = lax.rem(y + t, Y)
        remote(mine, mine, 14, (yy * Z + z) * C + c, m)
        remote(out_v.at[c, y], out_v.at[c, y], 14, (yy * Z + z) * C + c, m, True)

    each(1, Y, ag_y)

    @pl.when(jnp.logical_not(conc))
    def _():
        wait_in(recv_r, 2, True)
        wait_in(recv_t, 2)
        flat_rows()
        wait_in(recv_g, 13)

    wait_in(send_y.at[pl.ds(0, Y - 1)], 14)
    wait_in(out_v.at[0, pl.ds(0, Y - 1)], 14, True)
    myhalf = out_w.at[pl.ds(pl.multiple_of(c * hrows, 16), hrows), :]
    remote(myhalf, myhalf, 15, mate, m)
    remote(out_v.at[c], out_v.at[c], 15, mate, m, True)

    sel = onehot((iota((16, W), 1) & 15) == iota((16, W), 0))
    lists = dot(sel, entries(0, NS), ((1,), (1,)))
    cnt8 = lists[0:8, :]
    slot_row = lists[8:9, :]
    grads = recv_g[...].reshape(NS, W)
    QR = G * 16

    def update(i):
        row = iota((QR, 1), 0)
        slot_id = (lax.shift_right_logical(row, 3) + i * (QR // 8)).astype(F32)
        cnt = jnp.broadcast_to(cnt8[None], (QR // 8, 8, NS)).reshape(QR, NS)
        wide = jnp.where(slot_row == slot_id, cnt, 0.0).astype(BF)
        grad = dot(wide, grads)
        src_rows = rmat[pl.ds(pl.multiple_of(i * G, G), G), :]
        wide_s = jnp.broadcast_to(src_rows[:, None, :], (G, 16, W)).reshape(QR, W)
        pick_s = iota((QR, W), 1) == (iota((QR, W), 0) & 15) + 96
        st = jnp.sum(jnp.where(pick_s, wide_s, 0.0), axis=1, keepdims=True)
        st = st + jnp.sum(grad * grad, axis=1, keepdims=True) * (1.0 / W)
        old = recv_t[i].reshape(QR, W).astype(F32)
        new = old - learn_rate * grad / (jnp.sqrt(st) + epsilon)
        pick_o = iota((QR, W), 1) == (iota((QR, W), 0) & 7)
        st8 = jnp.sum(jnp.where(pick_o, st, 0.0).reshape(QR // 8, 8, W), axis=1)
        for q in range(Y):
            out_t[pl.ds(pl.multiple_of((q * Z + i) * 32, 32), 32), :] = new[q * 32 : (q + 1) * 32]
            out_s[q, i] = st8[q * 4 : (q + 1) * 4]

    each(0, Z, update)

    wait_in(recv_c, 15)
    wait_in(vec_c, 15, True)

    wait_out(mid_r.at[pl.ds(0, G - 1)], 0, True)
    wait_out(mid_t.at[pl.ds(0, G - 1)], 0)
    wait_out(mid_g.at[pl.ds(0, G - 1)], 9)
    wait_out(send_p.at[pl.ds(0, G - 1)], 4)
    wait_out(slots.at[pl.ds(0, M - 1)], 5)
    wait_out(lbuf.at[pl.ds(0, M - 1)], 3, True)
    wait_out(send_c, 6)
    wait_out(vec_c, 6, True)
    wait_out(part_s.at[pl.ds(0, M - 1)], 7)
    wait_out(send_y.at[pl.ds(0, Y - 1)], 8)
    wait_out(vec_y.at[pl.ds(0, Y - 1)], 8, True)
    wait_out(send_z.at[pl.ds(0, Z - 1)], 10)
    wait_out(vec_z.at[pl.ds(0, Z - 1)], 10, True)
    wait_out(send_z.at[pl.ds(0, Z - 1)], 12)
    wait_out(send_y.at[pl.ds(0, Y - 1)], 14)
    wait_out(out_v.at[0, pl.ds(0, Y - 1)], 14, True)
    wait_out(recv_c, 15)
    wait_out(vec_c, 15, True)

    @pl.when(conc)
    def _():
        if K > 1:
            wait_out(recv_r.at[pl.ds(0, K - 1)], 1, True)
            wait_out(recv_t.at[pl.ds(0, K - 1)], 1)
            wait_out(send_h.at[pl.ds(0, K - 1)], 11)
        for _ in range(M - 1):
            wait_out(recv_r, 2, True)
            wait_out(recv_t, 2)
            wait_out(recv_g, 13)
        wait_out(pooled.at[pl.ds(0, Z - 1)], 3)

    @pl.when(jnp.logical_not(conc))
    def _():
        wait_out(recv_r.at[pl.ds(0, K)], 1, True)
        wait_out(recv_t.at[pl.ds(0, K)], 1)
        wait_out(send_h, 11)


def local_step(
    dense_input,
    labels,
    table,
    adagrad_state,
    new_owner,
    bag_owner,
    bag_slot,
    bag_offsets,
    bag_length,
    w_first,
    b_first,
    w_out,
):
    blocks = table.shape[0]
    samples = dense_input.shape[0]
    hidden = w_first.shape[1]
    S = Shape(lax.axis_size("dp"), lax.axis_size("mp"), blocks, samples, hidden)
    C, Y, Z, M, K, G, N = S.C, S.Y, S.Z, S.M, S.K, S.G, S.N
    R2 = K * G * 8
    V = pltpu.VMEM
    vmem = pl.BlockSpec(memory_space=pltpu.VMEM)
    hrows = 512 // C
    out_t, out_s, out_w, out_v = pl.pallas_call(
        functools.partial(kernel, S),
        out_shape=(
            jax.ShapeDtypeStruct((blocks * 8, W), F32),
            jax.ShapeDtypeStruct((Y, Z, 4, W), F32),
            jax.ShapeDtypeStruct((512, hidden), BF),
            jax.ShapeDtypeStruct((C, Y, S.V, W), F32),
        ),
        in_specs=[vmem] * 12,
        out_specs=(vmem,) * 4,
        scratch_shapes=[
            V((2 * S.T * 8, W), F32),
            V((G, K, 16, W), BF),
            V((G, K, 1, W), F32),
            V((G, K, 16, W), BF),
            V((G, K, 1, W), F32),
            V((Z, G, 16, W), BF),
            V((Z, G, 1, W), F32),
            V((N, W), F32),
            V((Z, G * 8, W), BF),
            V((K, G * 8, W), BF),
            V((G, K * 8, W), BF),
            V((M, G, K * 8, W), BF),
            V((M, 8, samples), F32),
            V((samples, hidden), F32),
            V((samples, hidden), F32),
            V((4, samples, W), BF),
            V((M, R2, W), BF),
            V((M, R2, W), BF),
            V((G, K * 8, W), BF),
            V((G, K * 8, W), BF),
            V((K, G * 8, W), BF),
            V((Z, G * 8, W), BF),
            V((hrows, hidden), BF),
            V((hrows, hidden), F32),
            V((hrows, hidden), BF),
            V((Y, S.RY, hidden), BF),
            V((hrows, hidden), F32),
            V((Y, S.RY, hidden), BF),
            V((Z, S.pr, S.pc), BF),
            V((Z, S.pr, S.pc), BF),
            V((C, Y, S.V, W), F32),
            V((Y, S.V, W), F32),
            V((Y, S.V, W), F32),
            V((S.V, W), F32),
            V((Z, S.V, W), F32),
            pltpu.SemaphoreType.DMA((16,)),
            pltpu.SemaphoreType.DMA((16,)),
            pltpu.SemaphoreType.DMA((16,)),
            pltpu.SemaphoreType.DMA((16,)),
        ],
        compiler_params=pltpu.CompilerParams(
            collective_id=0, has_side_effects=True, vmem_limit_bytes=56 * 1024 * 1024
        ),
    )(
        new_owner.reshape(1, blocks),
        bag_owner.reshape(1, 3 * samples),
        bag_slot.reshape(1, 3 * samples),
        bag_offsets,
        bag_length.reshape(1, 3 * samples),
        dense_input,
        labels.reshape(1, samples),
        table.reshape(blocks * 8, W),
        adagrad_state,
        w_first,
        b_first.reshape(1, hidden),
        w_out.reshape(1, hidden),
    )
    vecs = out_v.reshape(C, hidden)
    return (
        out_t.reshape(blocks, 8, W),
        out_s.reshape(blocks, W)[:, :8],
        out_w,
        vecs[0],
        vecs[1],
    )


def solution(mesh):
    placed = (
        P("dp", None),
        P("dp"),
        P("dp", None, None),
        P("dp", None),
        P("dp"),
        P("dp", None),
        P("dp"),
        P("dp", None),
        P("dp"),
        P(None, "mp"),
        P("mp"),
        P("mp"),
    )
    return jax.shard_map(
        local_step,
        mesh=mesh,
        in_specs=placed,
        out_specs=(P("dp", None, None), P("dp", None), P(None, "mp"), P("mp"), P("mp")),
        check_vma=False,
    )
```

time: 847 us -> 118 us (0.14)
  blocking collectives: 525 us -> 0 us
  waiting for transfers between devices: 139 us -> 0 us
  Pallas kernels: 0 us -> 107 us
  starting transfers between devices: 64.5 us -> 0 us
  matrix products: 43.2 us -> 0 us
  local copies, waits for them, and re-layouts: 47 us -> 9.02 us
  between operations: 14.5 us -> 0.67 us
    psum x2 -> x0, blocking collectives: 525 us -> none  [the longest x1 517 us: local(): sum_w1, sum_w2, sum_b1 = lax.psum((term_w1, term_w2, term_b1), 'dp')]
    pallas_call x0 -> x1, Pallas kernels: none -> 107 us  [local_step(): pl.pallas_call(functools.partial(kernel, S), out_shape=(jax.ShapeDtypeStr...]
    all_to_all x5 -> x0, waiting for transfers between devices: 93.9 us -> none  [the longest x1 53.2 us: local(): lax.all_to_all(send_rows.reshape(peer_count, slot_cap, rows_blk, emb_widt...]
    all_to_all x5 -> x0, starting transfers between devices: 64.5 us -> none  [the longest x1 20.6 us: local(): lax.all_to_all(send_state.reshape(peer_count, slot_cap, rows_blk), 'dp',...]
    psum x1 -> x0, waiting for transfers between devices: 45.5 us -> none  [local(): lax.psum(part_input.astype(jnp.bfloat16), 'mp').astype(jnp.float32)]
    dot_general x11 -> x0, matrix products: 43.2 us -> none  [the longest x3 23 us: add_group(): lax.dot_general(counts, group_pair[1], (((0,), (0,)), ((), ())), precisio...]
    scatter x5 -> x0, local copies, waits for them, and re-layouts: 37 us -> none  [the longest x1 25.5 us: local(): send_rows = jnp.zeros((peer_count * slot_cap, rows_blk, emb_width), jnp.f...]
  transfers between devices with their start and end apart: 6 -> 0, of which waited for: 5 -> 0; matrix products, arithmetic and copies ran while one was open for 4% -> 0% of each run, Pallas kernels for 0% -> 0%
where the time goes in v1:
time: 118 us; the launch traced here: 116 us
  Pallas kernels  107 us (91%)
  local copies, waits for them, and re-layouts  9.02 us (8%)
    pallas_call x1, Pallas kernels, local_step(): pl.pallas_call(functools.partial(kernel, S), out_shape=(jax.ShapeDtypeStr...  107 us
    unnamed x17, local copies, waits for them, and re-layouts  7.29 us

profile of v1, /device:TPU:1, one launch (start us, length us, event | category | flops | bytes accessed | tf_op | source)
XLA Modules:
  0.0 116.2 jit_solution(1954103179792910468)
XLA Ops:
  0.6 0.0 copy-start.4
  0.6 0.0 copy-start.2
  0.7 0.7 copy-done.4
  1.3 0.0 copy-start.5
  1.3 0.6 reshape.47.bslot_ref
  1.9 0.1 copy-done.5
  2.0 0.6 reshape.48.blen_ref
  2.6 0.0 copy-done.2
  2.6 0.0 copy-start.1
  2.6 0.8 copy.18.state_ref
  3.4 0.0 copy-done.1
  3.4 0.8 copy.17.boff_ref
  4.2 106.5 %shard_map.155 = (f32[2048,128]{1,0:T(8,128)}, f32[4,16,4,128]{3,2,1,0:T(4,128)}, bf16[512,1024]{1,0:T(8,128)(2,1)}, f32[2,4,2,128]{3,2,1,0:T(2,128)}) custom-call(s32[1,256]{1,0:T(1,128)} %bitcast.19, s32[1,384]{1,0:T(1,128)} %bitcast.18, s32[1,384]{1,0:T(1,128)} %reshape.47.bslot_ref, s32[384,16]{1,0:T(8,128)} %copy.17.boff_ref, ...), custom_call_target="tpu_custom_call" | custom-call | tf_op jit(solution)/shard_map/pallas_call | solution.py:637
  110.7 0.0 copy-start.3
  110.7 1.6 %copy.20 = f32[256,8]{0,1:T(8,128)} copy(f32[256,8]{1,0:T(8,128)} %bitcast.13) | data formatting | bytes 16384
  112.3 0.0 copy-done.3
  112.3 0.6 fusion
  112.9 0.0 copy-start
  112.9 2.4 %copy.23 = f32[256,8,128]{2,1,0:T(8,128)} copy(f32[256,8,128]{2,1,0:T(8,128)} %bitcast.12) | data formatting | bytes 2097152
  115.2 0.0 copy-done
  115.2 1.0 copy.24
Async XLA Ops:
  0.6 0.7 copy-start.4
  0.6 1.9 %copy-start.2 = (f32[256,8]{0,1:T(8,128)S(1)}, f32[256,8]{0,1:T(8,128)}, u32[]{:S(2)}) copy-start(f32[256,8]{0,1:T(8,128)} %param.15) | copy-start | bytes 24580
  1.3 0.7 copy-start.5
  2.6 0.8 copy-start.1
  110.7 1.6 %copy-start.3 = (f32[2,4,2,128]{3,2,1,0:T(2,128)S(1)}, f32[2,4,2,128]{3,2,1,0:T(2,128)}, u32[]{:S(2)}) copy-start(f32[2,4,2,128]{3,2,1,0:T(2,128)} %get-tuple-element.12) | copy-start | bytes 24580
  112.9 2.4 %copy-start = (bf16[512,1024]{1,0:T(8,128)(2,1)S(1)}, bf16[512,1024]{1,0:T(8,128)(2,1)}, u32[]{:S(2)}) copy-start(bf16[512,1024]{1,0:T(8,128)(2,1)} %get-tuple-element.22) | copy-start | bytes 3145732

commit v2 on v1

v2 whole, which is shorter than its diff:
```python
import functools

import jax
import jax.numpy as jnp
from jax import lax
from jax.experimental import pallas as pl
from jax.experimental.pallas import tpu as pltpu
from jax.sharding import PartitionSpec as P

MESH = pl.DeviceIdType.MESH
BF = jnp.bfloat16
F32 = jnp.float32
I32 = jnp.int32
learn_rate = 0.01
epsilon = 1e-08
W = 128


def iota(shape, dim):
    return lax.broadcasted_iota(I32, shape, dim)


def dot(a, b, dims=((1,), (0,)), exact=False):
    return lax.dot_general(
        a,
        b,
        (dims, ((), ())),
        precision=lax.Precision.HIGHEST if exact else None,
        preferred_element_type=F32,
    )


def log2(n):
    return n.bit_length() - 1


def onehot(mask):
    return jnp.where(mask, 1.0, 0.0).astype(BF)


def to_col(row, rows, pick):
    return jnp.sum(jnp.where(pick, row, 0.0), axis=1, keepdims=True)


class Shape:
    def __init__(self, dp, mp, blocks, samples, hidden):
        self.C = 2
        self.Y = 4 if dp == 128 else 2
        self.Z = dp // (self.C * self.Y)
        self.M = mp
        self.K = self.Z // mp
        self.G = self.Y * self.C
        self.N = dp
        self.NB = blocks
        self.B = samples
        self.HL = hidden
        self.T = self.G * self.K
        self.RY = 512 // (self.C * self.Y)
        self.RG = min(self.Z, self.RY // 16)
        self.CG = self.Z // self.RG
        self.pr = self.RY // self.RG
        self.Q = 2
        self.HQ = hidden // self.Q
        self.pc = self.HQ // self.CG
        self.V = hidden // (W * self.Y)


def kernel(
    S,
    *refs,
):
    given, rest = refs[:12], refs[12:]
    held, inner = rest[-12:], rest[:-12]
    run(S, given, held, *inner)


def run(
    S,
    given,
    held,
    out_t,
    out_d,
    out_s,
    out_w,
    out_v,
    stage_s,
    stage_t,
    send_t,
    send_r,
    mid_t,
    mid_r,
    mid_q,
    recv_t,
    recv_r,
    pooled,
    mid_p,
    send_p,
    slots,
    lbuf,
    act,
    slope,
    feat,
    from_slot,
    to_slot,
    swap_ref,
    inputs,
    part_s,
    recv_x,
    send_h,
    recv_g,
    send_c,
    keep_c,
    recv_c,
    send_y,
    keep_y,
    recv_y,
    send_z,
    recv_z,
    vec,
    vec_c,
    vec_y,
    vec_ys,
    vec_z,
    ss,
    rs,
    sr,
    rr,
    in_sem,
):
    (owner_ref, bown_ref, bslot_ref, boff_ref, blen_ref, dense_ref, label_ref, table_ref, state_ref, w_ref, b_ref, wo_ref) = held
    C, Y, Z, M, K, G, N, NB, B, HL, T = S.C, S.Y, S.Z, S.M, S.K, S.G, S.N, S.NB, S.B, S.HL, S.T
    B3 = 3 * B
    NS = N * 8
    lY, lZ, lM, lK, lG = log2(Y), log2(Z), log2(M), log2(K), log2(G)
    me = lax.axis_index("dp")
    m = lax.axis_index("mp")
    c = lax.rem(me, C)
    z = lax.rem(me // C, Z)
    y = me // (C * Z)
    g = y * C + c
    half = M // 2
    home = lax.rem(z + half * c, M)
    conc = home == m
    base_z = lax.rem(m + M - half * c, M)

    def dp_of(gg, zz):
        return ((gg // C) * Z + zz) * C + lax.rem(gg, C)

    def remote(src, dst, i, dp, mp, small=False):
        pltpu.make_async_remote_copy(
            src_ref=src,
            dst_ref=dst,
            send_sem=(sr if small else ss).at[i],
            recv_sem=(rr if small else rs).at[i],
            device_id=(dp, mp),
            device_id_type=MESH,
        ).start()

    def local(src, dst, i, small=False):
        pltpu.make_async_copy(src, dst, (rr if small else rs).at[i]).start()

    def wait_in(ref, i, small=False):
        pltpu.make_async_copy(ref, ref, (rr if small else rs).at[i]).wait()

    def wait_out(ref, i, small=False):
        pltpu.make_async_copy(ref, ref, (sr if small else ss).at[i]).wait()

    ins = {}
    outs = []

    def take(name):
        ins.pop(name)()

    def sent(ref, i, small=False):
        outs.append(lambda: wait_out(ref, i, small))

    def sent_if(cond, body):
        outs.append(lambda: pl.when(cond)(body))

    def each(lo, hi, body):
        def step(t, carry):
            body(t)
            return carry

        lax.fori_loop(lo, hi, step, 0)

    loads = [pltpu.make_async_copy(a, h, in_sem.at[i]) for i, (a, h) in enumerate(zip(given, held))]
    for load in loads:
        load.start()

    barrier = pltpu.get_barrier_semaphore()

    def greet(dp, mp):
        pl.semaphore_signal(barrier, inc=1, device_id=(dp, mp), device_id_type=MESH)

    ys = [lax.rem(y + i, Y) for i in range(Y)]
    cs = [c, 1 - c]
    ms = [lax.rem(m + i, M) for i in range(M)]
    steps = [(i, j, k) for i in range(Y) for j in range(C) for k in range(M) if (i, j, k) != (0, 0, 0)]
    steps.sort(key=lambda a: -(min(a[0], Y - a[0]) + min(a[2], M - a[2])))
    near = [((ys[i] * Z + z) * C + cs[j], ys[i] * C + cs[j], ms[k]) for i, j, k in steps]

    def along_z(body):
        def step(i):
            away = (i + 1) // 2
            body(lax.rem(z + Z // 2 + Z + away * (1 - 2 * lax.rem(i, 2)), Z))

        each(0, Z - 1, step)

    for dp, _, mm in near:
        greet(dp, mm)
    along_z(lambda zz: greet(dp_of(g, zz), m))

    for load in loads[:9]:
        load.wait()

    def target_of(tt):
        gg = lax.shift_right_logical(tt, lK)
        kk = tt & (K - 1)
        yy = lax.shift_right_logical(gg, 1)
        cc = gg & 1
        zz = ((m + M - half * cc) & (M - 1)) + M * kk
        return (yy * Z + zz) * C + cc

    own_row = owner_ref[...].astype(F32)
    own_col = to_col(own_row, NB, iota((NB, NB), 0) == iota((NB, NB), 1))
    rank_row = jnp.sum(
        jnp.where((own_col == own_row) & (iota((NB, NB), 0) < iota((NB, NB), 1)), 1.0, 0.0),
        axis=0,
        keepdims=True,
    )
    rows2 = iota((2 * T, 1), 0)
    want = target_of(lax.shift_right_logical(rows2, 1)).astype(F32)
    pick_f = jnp.where((own_row == want) & (rank_row == (rows2 & 1).astype(F32)), 1.0, 0.0)
    pick = pick_f.astype(BF)
    for r in range(8):
        low = table_ref[pl.ds(r, NB, stride=8), :].astype(BF)
        stage_t[pl.ds(r, 2 * T, stride=8), :] = dot(pick, low)
    send_t[...] = stage_t[...].astype(BF).reshape(G, K, 16, W)

    bo = bown_ref[...]
    bo_row = bo.astype(F32)
    bo_col = to_col(bo_row, B3, iota((B3, B3), 0) == iota((B3, B3), 1))
    brank_row = jnp.sum(
        jnp.where((bo_col == bo_row) & (iota((B3, B3), 0) < iota((B3, B3), 1)), 1.0, 0.0),
        axis=0,
        keepdims=True,
    )
    slot_nat = bslot_ref[...].reshape(1, B3)
    sy = lax.shift_right_logical(slot_nat, lZ + 2)
    sz = lax.shift_right_logical(slot_nat, 2) & (Z - 1)
    slot_z = ((sz * Y + sy) * 4 + (slot_nat & 3)).astype(F32)
    live = iota((16, B3), 0) < blen_ref[...].reshape(1, B3)
    offs = jnp.where(live, boff_ref[...], -1)
    cnts = [jnp.sum(jnp.where(offs == o, 1.0, 0.0), axis=0, keepdims=True) for o in range(8)]
    line = iota((8, B3), 0)
    cnt8 = jnp.zeros((8, B3), F32)
    for o in range(8):
        cnt8 = jnp.where(line == o, cnts[o], cnt8)
    one16 = jnp.concatenate([cnt8, jnp.where(line == 0, slot_z, 0.0)], axis=0)
    req = jnp.concatenate([one16] * 8, axis=0)
    req = jnp.where(lax.shift_right_logical(iota((W, B3), 0), 4).astype(F32) == brank_row, req, 0.0).astype(BF)
    want_t = target_of(iota((T, 1), 0)).astype(F32)
    rows = dot(onehot(bo_row == want_t), req, ((1,), (1,)))
    for p in range(2):
        pad = [jnp.zeros((96 + 8 * p, NB), F32), state_ref[...], jnp.zeros((24 - 8 * p, NB), F32)]
        pick_p = jnp.where((own_row == want_t) & (rank_row == float(p)), 1.0, 0.0)
        rows = rows + dot(pick_p, jnp.concatenate(pad, axis=0), ((1,), (1,)), exact=True)
    for t in range(T):
        send_r[t // K, t % K] = rows[t : t + 1, :]

    pl.semaphore_wait(barrier, (M * G - 1) + (Z - 1))

    local(send_r.at[g], mid_r.at[g], 0, True)
    local(send_t.at[g], mid_t.at[g], 0)

    def fwd_a(t):
        gg = lax.rem(g + t, G)
        remote(send_r.at[gg], mid_r.at[g], 0, dp_of(gg, z), m, True)
        remote(send_t.at[gg], mid_t.at[g], 0, dp_of(gg, z), m)

    each(1, G, fwd_a)
    sent(mid_r.at[pl.ds(0, G - 1)], 0, True)
    sent(mid_t.at[pl.ds(0, G - 1)], 0)
    ins["mid"] = lambda: (wait_in(mid_r, 0, True), wait_in(mid_t, 0))
    take("mid")
    for t in range(T):
        mid_q[t % K, pl.ds(t // K, 1), :] = mid_r[t // K, t % K]

    def fwd_b(k):
        zz = base_z + M * k

        @pl.when(zz != z)
        def _():
            remote(mid_q.at[k], recv_r.at[z], 1, dp_of(g, zz), m, True)
            remote(mid_t.at[:, k], recv_t.at[z], 1, dp_of(g, zz), m)

        @pl.when(zz == z)
        def _():
            local(mid_q.at[k], recv_r.at[z], 1, True)
            local(mid_t.at[:, k], recv_t.at[z], 1)

    each(0, K, fwd_b)

    def fwd_b_sent(n):
        if n:
            wait_out(recv_r.at[pl.ds(0, n)], 1, True)
            wait_out(recv_t.at[pl.ds(0, n)], 1)

    sent_if(conc, lambda: fwd_b_sent(K - 1))
    sent_if(jnp.logical_not(conc), lambda: fwd_b_sent(K))

    def wait_blocks():
        wait_in(recv_r, 1, True)
        wait_in(recv_t, 1)

    ins["blocks"] = lambda: pl.when(conc)(wait_blocks)

    oc = bo & 1
    oz = lax.shift_right_logical(bo, 1) & (Z - 1)
    oy = lax.shift_right_logical(bo, 1 + lZ)
    om = (oz + half * oc) & (M - 1)
    ok = lax.shift_right_logical(oz, lM)
    place = (((om * G + oy * C + oc) * K + ok) * 8).astype(F32) + brank_row
    pcol, prow = [], []
    for f in range(3):
        col = to_col(place, B, iota((B, B3), 1) == 3 * iota((B, B3), 0) + f)
        pcol.append(col)
        prow.append(jnp.sum(jnp.where(iota((B, B), 0) == iota((B, B), 1), col, 0.0), axis=0, keepdims=True))

    low16 = iota((W, W), 0) & 15
    tile_c = onehot(low16 == (iota((W, W), 1) & 7))
    tile_s = onehot(low16 == 8)

    CH = min(NS, 2 * G * 8)

    def entries(i, n):
        row = iota((n, N), 0) + i * n
        src = onehot(lax.shift_right_logical(row, 3) == iota((n, N), 1))
        wide = dot(src, jnp.where(iota((N, W), 1) < 96, recv_r[...].reshape(N, W), 0.0).astype(BF))
        keep = lax.shift_right_logical(iota((n, W), 1), 4) == (iota((n, W), 0) & 7)
        return jnp.where(keep, wide, 0.0).astype(BF)

    R2 = K * G * 8
    ro = iota((R2, R2), 0)
    ri = iota((R2, R2), 1)
    for i, (a, b) in enumerate(((ro, ri), (ri, ro))):
        swap_ref[i] = onehot(
            (lax.shift_right_logical(a, lK + 3) == (lax.shift_right_logical(b, 3) & (G - 1)))
            & ((lax.shift_right_logical(a, 3) & (K - 1)) == lax.shift_right_logical(b, lG + 3))
            & ((a & 7) == (b & 7))
        )
    for f in range(3):
        from_slot[f] = onehot(iota((B, NS), 1).astype(F32) == pcol[f])
        for q in range(M):
            to_slot[q, :, f * B : (f + 1) * B] = onehot((iota((R2, B), 0) + q * R2).astype(F32) == prow[f])

    take("blocks")

    def cast_r():
        each(1, M, lambda t: remote(recv_r, recv_r, 2, me, lax.rem(m + t, M), True))

    def cast_r_sent():
        for _ in range(M - 1):
            wait_out(recv_r, 2, True)

    pl.when(conc)(cast_r)
    sent_if(conc, cast_r_sent)
    ins["cast_r"] = lambda: pl.when(jnp.logical_not(conc))(lambda: wait_in(recv_r, 2, True))

    @pl.when(conc)
    def _():
        def pool(step):
            n = NS // CH
            away = (step + 1) // 2
            i = lax.rem(z // (Z // n) + n // 2 + n + away * (1 - 2 * lax.rem(step, 2)), n)
            ent = entries(i, CH)
            cnt = dot(ent, tile_c)
            slt = dot(ent, tile_s)
            group = lax.shift_right_logical(iota((CH, W), 1), 3)
            parts = [
                jnp.where(slt == (group + 16 * q).astype(F32), cnt, 0.0).astype(BF) for q in range(NB // 16)
            ]
            wide = jnp.concatenate(parts, axis=1) if len(parts) > 1 else parts[0]
            got = dot(wide, recv_t[...].reshape(NB * 8, W))
            per = CH // (G * 8)
            pooled[pl.ds(i * per, per)] = got.astype(BF).reshape(per, G * 8, W)

            def send(q):
                zz = i * per + q

                @pl.when(zz != z)
                def _():
                    remote(pooled.at[zz], mid_p.at[z // M], 3, dp_of(g, zz), m)

                @pl.when(zz == z)
                def _():
                    local(pooled.at[zz], mid_p.at[z // M], 3)

            each(0, per, send)

        each(0, NS // CH, pool)

    sent_if(conc, lambda: wait_out(pooled.at[pl.ds(0, Z - 1)], 3))
    ins["pooled"] = lambda: wait_in(mid_p, 3)

    take("pooled")
    send_p[...] = dot(swap_ref[0], mid_p[...].reshape(R2, W)).astype(BF).reshape(G, K * 8, W)
    local(send_p.at[g], slots.at[m * G + g], 4)

    for dp, gg, mm in near:
        remote(send_p.at[gg], slots.at[m * G + g], 4, dp, mm)
    sent(slots.at[pl.ds(0, M * G - 1)], 4)
    ins["slots"] = lambda: wait_in(slots, 4)
    take("slots")

    for load in loads[9:]:
        load.wait()
    table_s = slots[...].reshape(NS, W)
    feat[0] = dense_ref[...]
    for f in range(3):
        feat[f + 1] = dot(from_slot[f], table_s).astype(BF)
    features = jnp.concatenate([feat[i] for i in range(4)], axis=1)
    pre = dot(features, w_ref[...]) + b_ref[...]
    sig = jax.nn.sigmoid(pre)
    active = pre * sig
    act[...] = active
    slope[...] = sig * (1.0 + pre * (1.0 - sig)) * wo_ref[...]
    part = jnp.sum(active * wo_ref[...], axis=1, keepdims=True)
    eye_b = iota((B, B), 0) == iota((B, B), 1)
    part_row = jnp.sum(jnp.where(eye_b, part, 0.0), axis=0, keepdims=True)
    lbuf[m] = jnp.broadcast_to(part_row, (8, B))
    each(1, M, lambda t: remote(lbuf.at[m], lbuf.at[m], 3, me, lax.rem(m + t, M), True))
    sent(lbuf.at[pl.ds(0, M - 1)], 3, True)
    ins["logits"] = lambda: wait_in(lbuf.at[pl.ds(0, M - 1)], 3, True)
    take("logits")

    total = lbuf[0]
    for i in range(1, M):
        total = total + lbuf[i]
    lgrad_row = jax.nn.sigmoid(total[0:1, :]) - label_ref[...].astype(F32)
    lgrad = to_col(lgrad_row, B, eye_b)
    grad_pre = lgrad * slope[...]
    grad_low = grad_pre.astype(BF)
    hrows = 512 // C
    other = 1 - c
    mate = me + 1 - 2 * c

    def term_of(i, blk):
        return dot(feat[i], blk, ((0,), (0,)))

    for q in range(S.Q):
        low_q = grad_low[:, q * S.HQ : (q + 1) * S.HQ]
        for h in range(C):

            @pl.when(c != h)
            def _():
                for i in range(2):
                    send_c[q, pl.ds(i * W, W), :] = term_of(2 * h + i, low_q).astype(BF)

            @pl.when(c == h)
            def _():
                for i in range(2):
                    keep_c[q, pl.ds(i * W, W), :] = term_of(2 * h + i, low_q)

        remote(send_c.at[q], recv_c.at[q], 16 + q, mate, m)
        sent(send_c.at[q], 16 + q)
        ins["core", q] = lambda q=q: wait_in(recv_c.at[q], 16 + q)

    for f in range(3):
        term = dot(grad_low, w_ref[pl.ds((f + 1) * W, W), :], ((1,), (1,)))
        inputs[pl.ds(f * B, B), :] = term.astype(BF)
    for q in range(S.Q):
        take(("core", q))
        keep_y[q] = keep_c[q] + recv_c[q].astype(F32)
        send_y[q] = keep_y[q].astype(BF).reshape(Y, S.RY, S.HQ)

        def to_y(t):
            yy = lax.rem(y + t, Y)
            remote(send_y.at[q, yy], recv_y.at[q, y], 18 + q, (yy * Z + z) * C + c, m)

        each(1, Y, to_y)
        sent(send_y.at[q, pl.ds(0, Y - 1)], 18 + q)
        ins["dense_y", q] = lambda q=q: wait_in(recv_y.at[q, pl.ds(0, Y - 1)], 18 + q)
    for q in range(M):
        part_s[q] = dot(to_slot[q], inputs[...]).astype(BF).reshape(G, K * 8, W)

    local(part_s.at[m, g], recv_x.at[m * G + g], 7)
    for dp, gg, mm in near:
        remote(part_s.at[mm, gg], recv_x.at[m * G + g], 7, dp, mm)
    sent(recv_x.at[pl.ds(0, M * G - 1)], 7)
    ins["bags_x"] = lambda: wait_in(recv_x, 7)

    b1 = jnp.sum(grad_pre, axis=0, keepdims=True)
    w2 = jnp.sum(lgrad * act[...], axis=0, keepdims=True)
    for i, row in enumerate((b1, w2)):
        for j in range(HL // W):
            vec[i, j // S.V, pl.ds(j % S.V, 1), :] = row[:, j * W : (j + 1) * W]

    remote(vec.at[other], vec_c, 6, mate, m, True)
    sent(vec_c, 6, True)
    ins["core_v"] = lambda: wait_in(vec_c, 6, True)


    take("core_v")
    vec[c] = vec[c] + vec_c[...]

    def to_y_vec(t):
        yy = lax.rem(y + t, Y)
        remote(vec.at[c, yy], vec_y.at[y], 8, (yy * Z + z) * C + c, m, True)

    each(1, Y, to_y_vec)
    sent(vec_y.at[pl.ds(0, Y - 1)], 8, True)
    ins["dense_yv"] = lambda: wait_in(vec_y.at[pl.ds(0, Y - 1)], 8, True)

    def dense_z(q):
        take(("dense_y", q))
        acc = keep_y[q, pl.ds(pl.multiple_of(y * S.RY, S.RY), S.RY), :]
        for t in range(1, Y):
            acc = acc + recv_y[q, lax.rem(y + t, Y)].astype(F32)
        for i in range(Z):
            r0, c0 = (i // S.CG) * S.pr, (i % S.CG) * S.pc
            send_z[q, i] = acc[r0 : r0 + S.pr, c0 : c0 + S.pc].astype(BF)
        local(send_z.at[q, z], recv_z.at[q, z], 20 + q)

        def to_z(zz):
            remote(send_z.at[q, zz], recv_z.at[q, z], 20 + q, dp_of(g, zz), m)

        along_z(to_z)
        sent(send_z.at[q, pl.ds(0, Z - 1)], 20 + q)
        ins["dense_z", q] = lambda: wait_in(recv_z.at[q], 20 + q)

    for q in range(S.Q):
        dense_z(q)

    take("bags_x")
    total = recv_x[pl.ds(0, G)].astype(F32)
    for i in range(1, M):
        total = total + recv_x[pl.ds(i * G, G)].astype(F32)
    send_h[...] = dot(swap_ref[1], total.astype(BF).reshape(R2, W)).astype(BF).reshape(K, G * 8, W)

    def grad_b(k):
        zz = base_z + M * k

        @pl.when(zz != z)
        def _():
            remote(send_h.at[k], recv_g.at[z], 11, dp_of(g, zz), m)

        @pl.when(zz == z)
        def _():
            local(send_h.at[k], recv_g.at[z], 11)

    each(0, K, grad_b)

    def grad_b_sent(n):
        if n:
            wait_out(send_h.at[pl.ds(0, n)], 11)

    sent_if(conc, lambda: grad_b_sent(K - 1))
    sent_if(jnp.logical_not(conc), lambda: grad_b_sent(K))
    ins["grads"] = lambda: pl.when(conc)(lambda: wait_in(recv_g, 11))


    take("dense_yv")
    accv = vec[c, y]
    for t in range(1, Y):
        accv = accv + vec_y[lax.rem(y + t, Y)]
    vec_ys[...] = accv
    local(vec_ys, vec_z.at[z], 10, True)
    along_z(lambda zz: remote(vec_ys, vec_z.at[z], 10, dp_of(g, zz), m, True))
    sent(vec_z.at[pl.ds(0, Z - 1)], 10, True)
    ins["dense_zv"] = lambda: wait_in(vec_z, 10, True)
    def cast_t():
        for h in range(2):
            part = recv_t.at[pl.ds(h * (Z // 2), Z // 2)]
            each(1, M, lambda t: remote(part, part, 2, me, lax.rem(m + t, M)))

    def cast_t_sent():
        for _ in range(M - 1):
            wait_out(recv_t, 2)

    pl.when(conc)(cast_t)
    sent_if(conc, cast_t_sent)
    ins["cast_t"] = lambda: pl.when(jnp.logical_not(conc))(lambda: wait_in(recv_t, 2))


    block0 = c * hrows + y * S.RY

    def gather_z(q):
        take(("dense_z", q))

        def add_z(i, carry):
            return carry + recv_z[q, i].astype(F32)

        acc = lax.fori_loop(0, Z, add_z, jnp.zeros((S.pr, S.pc), F32))
        r0 = pl.multiple_of(block0 + (z // S.CG) * S.pr, 16)
        c0 = pl.multiple_of(q * S.HQ + lax.rem(z, S.CG) * S.pc, W)
        out_w[pl.ds(r0, S.pr), pl.ds(c0, S.pc)] = acc.astype(BF)
        piece = out_w.at[pl.ds(r0, S.pr), pl.ds(c0, S.pc)]
        along_z(lambda zz: remote(piece, piece, 22 + q, dp_of(g, zz), m))
        sent(send_z.at[q, pl.ds(0, Z - 1)], 22 + q)
        ins["out_z", q] = lambda: wait_in(send_z.at[q, pl.ds(0, Z - 1)], 22 + q)


    for q in range(S.Q):
        gather_z(q)
    take("cast_r")
    sel = onehot((iota((16, W), 1) & 15) == iota((16, W), 0))
    lists = dot(sel, entries(0, NS), ((1,), (1,)))
    list8 = lists[0:8, :]
    slot_row = lists[8:9, :]
    take("grads")

    @pl.when(conc)
    def _():
        each(1, M, lambda t: remote(recv_g, recv_g, 13, me, lax.rem(m + t, M)))

    def grads_sent():
        for _ in range(M - 1):
            wait_out(recv_g, 13)

    sent_if(conc, grads_sent)
    ins["grads_x"] = lambda: pl.when(jnp.logical_not(conc))(lambda: wait_in(recv_g, 13))

    take("dense_zv")
    accv = vec_z[0]
    for i in range(1, Z):
        accv = accv + vec_z[i]
    out_v[c, y] = accv

    def ag_yv(t):
        yy = lax.rem(y + t, Y)
        remote(out_v.at[c, y], out_v.at[c, y], 14, (yy * Z + z) * C + c, m, True)

    each(1, Y, ag_yv)
    sent(out_v.at[0, pl.ds(0, Y - 1)], 14, True)
    ins["out_yv"] = lambda: wait_in(out_v.at[0, pl.ds(0, Y - 1)], 14, True)

    QR = G * 16

    def update(pair):
        for i in (2 * pair, 2 * pair + 1):
            update_one(i)

    def update_one(i):
        row = iota((QR, 1), 0)
        slot_id = (lax.shift_right_logical(row, 3) + i * (QR // 8)).astype(F32)
        cnt = jnp.broadcast_to(list8[None], (QR // 8, 8, NS)).reshape(QR, NS)
        wide = jnp.where(slot_row == slot_id, cnt, 0.0).astype(BF)
        grad = dot(wide, recv_g[...].reshape(NS, W))
        src_rows = recv_r[i]
        wide_s = jnp.broadcast_to(src_rows[:, None, :], (G, 16, W)).reshape(QR, W)
        pick_s = iota((QR, W), 1) == (iota((QR, W), 0) & 15) + 96
        st = jnp.sum(jnp.where(pick_s, wide_s, 0.0), axis=1, keepdims=True)
        st = st + jnp.sum(grad * grad, axis=1, keepdims=True) * (1.0 / W)
        low = recv_t[i].reshape(QR, W)
        step = (learn_rate * grad / (jnp.sqrt(st) + epsilon)).astype(BF)
        pick_o = iota((QR, W), 1) == (iota((QR, W), 0) & 7)
        st8 = jnp.sum(jnp.where(pick_o, st, 0.0).reshape(QR // 8, 8, W), axis=1)
        for q in range(Y):
            at = pl.ds(pl.multiple_of((q * Z + i) * 32, 32), 32)
            out_t[at, :] = low[q * 32 : (q + 1) * 32]
            out_d[at, :] = step[q * 32 : (q + 1) * 32]
            stage_s[pl.ds((q * Z + i) * 4, 4), :] = st8[q * 4 : (q + 1) * 4]

    for q in range(S.Q):
        take(("out_z", q))
        mine = out_w.at[pl.ds(pl.multiple_of(block0, 16), S.RY), pl.ds(q * S.HQ, S.HQ)]

        def ag_y(t):
            yy = lax.rem(y + t, Y)
            remote(mine, mine, 24 + q, (yy * Z + z) * C + c, m)

        each(1, Y, ag_y)
        sent(send_y.at[q, pl.ds(0, Y - 1)], 24 + q)
        ins["out_y", q] = lambda q=q: wait_in(send_y.at[q, pl.ds(0, Y - 1)], 24 + q)

    take("cast_t")
    take("grads_x")
    each(0, Z // 2, update)

    def gather_core(q):
        take(("out_y", q))
        part = out_w.at[pl.ds(pl.multiple_of(c * hrows, 16), hrows), pl.ds(q * S.HQ, S.HQ)]
        remote(part, part, 26 + q, mate, m)
        sent(send_c.at[q], 26 + q)
        ins["out_c", q] = lambda: wait_in(recv_c.at[q], 26 + q)

    for q in range(S.Q):
        gather_core(q)
    take("out_yv")
    remote(out_v.at[c], out_v.at[c], 15, mate, m, True)
    sent(vec_c, 15, True)
    ins["out_cv"] = lambda: wait_in(vec_c, 15, True)
    out_s[...] = jnp.transpose(stage_s[...])[0:8, :]
    take("out_cv")
    for q in range(S.Q):
        take(("out_c", q))
    assert not ins

    for done in outs:
        done()


def local_step(
    dense_input,
    labels,
    table,
    adagrad_state,
    new_owner,
    bag_owner,
    bag_slot,
    bag_offsets,
    bag_length,
    w_first,
    b_first,
    w_out,
):
    blocks = table.shape[0]
    samples = dense_input.shape[0]
    hidden = w_first.shape[1]
    S = Shape(lax.axis_size("dp"), lax.axis_size("mp"), blocks, samples, hidden)
    C, Y, Z, M, K, G, N = S.C, S.Y, S.Z, S.M, S.K, S.G, S.N
    R2 = K * G * 8
    V = pltpu.VMEM
    vmem = pl.BlockSpec(memory_space=pltpu.VMEM)
    hrows = 512 // C
    args = (
        new_owner.reshape(1, blocks),
        bag_owner.reshape(1, 3 * samples),
        bag_slot,
        bag_offsets.T,
        bag_length,
        dense_input,
        labels.reshape(1, samples),
        table.reshape(blocks * 8, W),
        adagrad_state.T,
        w_first,
        b_first.reshape(1, hidden),
        w_out.reshape(1, hidden),
    )
    out_t, out_d, out_s, out_w, out_v = pl.pallas_call(
        functools.partial(kernel, S),
        out_shape=(
            jax.ShapeDtypeStruct((blocks * 8, W), BF),
            jax.ShapeDtypeStruct((blocks * 8, W), BF),
            jax.ShapeDtypeStruct((8, blocks), F32),
            jax.ShapeDtypeStruct((512, hidden), BF),
            jax.ShapeDtypeStruct((C, Y, S.V, W), F32),
        ),
        in_specs=[pl.BlockSpec(memory_space=pltpu.HBM)] * 12,
        out_specs=(vmem,) * 5,
        scratch_shapes=[
            V((blocks, W), F32),
            V((2 * S.T * 8, W), F32),
            V((G, K, 16, W), BF),
            V((G, K, 1, W), F32),
            V((G, K, 16, W), BF),
            V((G, K, 1, W), F32),
            V((K, G, W), F32),
            V((Z, G, 16, W), BF),
            V((Z, G, W), F32),
            V((Z, G * 8, W), BF),
            V((K, G * 8, W), BF),
            V((G, K * 8, W), BF),
            V((M * G, K * 8, W), BF),
            V((M, 8, samples), F32),
            V((samples, hidden), F32),
            V((samples, hidden), F32),
            V((4, samples, W), BF),
            V((3, samples, S.N * 8), BF),
            V((M, R2, 3 * samples), BF),
            V((2, R2, R2), BF),
            V((3 * samples, W), BF),
            V((M, G, K * 8, W), BF),
            V((M * G, K * 8, W), BF),
            V((K, G * 8, W), BF),
            V((Z, G * 8, W), BF),
            V((S.Q, hrows, S.HQ), BF),
            V((S.Q, hrows, S.HQ), F32),
            V((S.Q, hrows, S.HQ), BF),
            V((S.Q, Y, S.RY, S.HQ), BF),
            V((S.Q, hrows, S.HQ), F32),
            V((S.Q, Y, S.RY, S.HQ), BF),
            V((S.Q, Z, S.pr, S.pc), BF),
            V((S.Q, Z, S.pr, S.pc), BF),
            V((C, Y, S.V, W), F32),
            V((Y, S.V, W), F32),
            V((Y, S.V, W), F32),
            V((S.V, W), F32),
            V((Z, S.V, W), F32),
            pltpu.SemaphoreType.DMA((32,)),
            pltpu.SemaphoreType.DMA((32,)),
            pltpu.SemaphoreType.DMA((32,)),
            pltpu.SemaphoreType.DMA((32,)),
            pltpu.SemaphoreType.DMA((12,)),
        ]
        + [V(a.shape, a.dtype) for a in args],
        compiler_params=pltpu.CompilerParams(
            collective_id=0, has_side_effects=True, vmem_limit_bytes=56 * 1024 * 1024
        ),
    )(*args)
    vecs = out_v.reshape(C, hidden)
    return (
        (out_t.astype(F32) - out_d.astype(F32)).reshape(blocks, 8, W),
        out_s.T,
        out_w,
        vecs[0],
        vecs[1],
    )


def solution(mesh):
    placed = (
        P("dp", None),
        P("dp"),
        P("dp", None, None),
        P("dp", None),
        P("dp"),
        P("dp", None),
        P("dp"),
        P("dp", None),
        P("dp"),
        P(None, "mp"),
        P("mp"),
        P("mp"),
    )
    return jax.shard_map(
        local_step,
        mesh=mesh,
        in_specs=placed,
        out_specs=(P("dp", None, None), P("dp", None), P(None, "mp"), P("mp"), P("mp")),
        check_vma=False,
    )
```

time: 118 us -> 99.7 us (0.84)
  Pallas kernels: 107 us -> 92.7 us
  local copies, waits for them, and re-layouts: 9.02 us -> 2.28 us
  other arithmetic: 0 us -> 2.36 us
    pallas_call x1, Pallas kernels: 107 us -> 92.7 us  [local_step(): pl.pallas_call(functools.partial(kernel, S), out_shape=(jax.ShapeDtypeStr...]
    unnamed x17 -> x8, local copies, waits for them, and re-layouts: 7.29 us -> 1.68 us
    reshape x0 -> x1, other arithmetic: none -> 2.36 us  [local_step(): (out_t.astype(F32) - out_d.astype(F32)).reshape(blocks, 8, W)]
where the time goes in v2:
time: 99.7 us; the launch traced here: 98 us
  Pallas kernels  92.7 us (93%)
  other arithmetic  2.36 us (2%)
  local copies, waits for them, and re-layouts  2.28 us (2%)
    pallas_call x1, Pallas kernels, local_step(): pl.pallas_call(functools.partial(kernel, S), out_shape=(jax.ShapeDtypeStr...  92.7 us
    reshape x1, other arithmetic, local_step(): (out_t.astype(F32) - out_d.astype(F32)).reshape(blocks, 8, W)  2.36 us

profile of v2, /device:TPU:1, one launch (start us, length us, event | category | flops | bytes accessed | tf_op | source)
XLA Modules:
  0.0 98.0 jit_solution(9816888943346209702)
XLA Ops:
  0.6 92.7 %shard_map.155 = (bf16[2048,128]{1,0:T(8,128)(2,1)}, bf16[2048,128]{1,0:T(8,128)(2,1)}, f32[8,256]{1,0:T(8,128)}, bf16[512,1024]{1,0:T(8,128)(2,1)}, f32[2,4,2,128]{3,2,1,0:T(2,128)}) custom-call(s32[1,256]{1,0:T(1,128)} %bitcast.22, s32[1,384]{1,0:T(1,128)} %bitcast.21, s32[384]{0:T(512)} %refs_2_.1, s32[16,384]{1,0:T(8,128)} %bitcast.14, s32[384]{0:T(512)} %refs_4_.1, ...), custom_call_target="tpu_custom_call" | custom-call | tf_op jit(solution)/shard_map/pallas_call | solution.py:742
  93.4 0.0 copy-start.2
  93.4 0.0 copy-start
  93.4 2.4 %subtract_bitcast_fusion = f32[256,8,128]{2,1,0:T(8,128)} fusion(bf16[2048,128]{1,0:T(8,128)(2,1)} %get-tuple-element.11, bf16[2048,128]{1,0:T(8,128)(2,1)} %get-tuple-element.10), kind=kLoop, calls=%fused_computation | loop fusion | flops 786432 | bytes 2097152 | tf_op jit(solution)/shard_map/reshape | solution.py:805
  95.7 0.0 copy-done.2
  95.7 0.0 copy-start.1
  95.7 0.6 fusion
  96.3 0.1 copy-done.1
  96.4 0.6 copy.19
  97.0 0.0 copy-done
  97.0 1.0 copy.20
Async XLA Ops:
  93.4 2.4 %copy-start.2 = (f32[2,4,2,128]{3,2,1,0:T(2,128)S(1)}, f32[2,4,2,128]{3,2,1,0:T(2,128)}, u32[]{:S(2)}) copy-start(f32[2,4,2,128]{3,2,1,0:T(2,128)} %get-tuple-element.14) | copy-start | bytes 24580
  93.4 3.7 %copy-start = (bf16[512,1024]{1,0:T(8,128)(2,1)S(1)}, bf16[512,1024]{1,0:T(8,128)(2,1)}, u32[]{:S(2)}) copy-start(bf16[512,1024]{1,0:T(8,128)(2,1)} %get-tuple-element.24) | copy-start | bytes 3145732
  95.7 0.7 copy-start.1

commit v3 on v2

--- a/solution.py
+++ b/solution.py
@@ -69,15 +69,16 @@
     S,
     *refs,
 ):
-    given, rest = refs[:12], refs[12:]
-    held, inner = rest[-12:], rest[:-12]
-    run(S, given, held, *inner)
+    given, results, rest = refs[:12], refs[12:17], refs[17:]
+    held, made, inner = rest[-17:-5], rest[-5:], rest[:-17]
+    run(S, given, held, results, *made, *inner)
 
 
 def run(
     S,
     given,
     held,
+    results,
     out_t,
     out_d,
     out_s,
@@ -100,6 +101,7 @@
     act,
     slope,
     feat,
+    feat_t,
     from_slot,
     to_slot,
     swap_ref,
@@ -126,6 +128,7 @@
     sr,
     rr,
     in_sem,
+    out_sem,
 ):
     (owner_ref, bown_ref, bslot_ref, boff_ref, blen_ref, dense_ref, label_ref, table_ref, state_ref, w_ref, b_ref, wo_ref) = held
     C, Y, Z, M, K, G, N, NB, B, HL, T = S.C, S.Y, S.Z, S.M, S.K, S.G, S.N, S.NB, S.B, S.HL, S.T
@@ -184,10 +187,6 @@
 
         lax.fori_loop(lo, hi, step, 0)
 
-    loads = [pltpu.make_async_copy(a, h, in_sem.at[i]) for i, (a, h) in enumerate(zip(given, held))]
-    for load in loads:
-        load.start()
-
     barrier = pltpu.get_barrier_semaphore()
 
     def greet(dp, mp):
@@ -207,12 +206,15 @@
 
         each(0, Z - 1, step)
 
+    along_z(lambda zz: greet(dp_of(g, zz), m))
+    loads = [pltpu.make_async_copy(a, h, in_sem.at[i]) for i, (a, h) in enumerate(zip(given, held))]
+    for load in loads:
+        load.start()
     for dp, _, mm in near:
         greet(dp, mm)
-    along_z(lambda zz: greet(dp_of(g, zz), m))
-
-    for load in loads[:9]:
-        load.wait()
+
+    for i in (0, 7):
+        loads[i].wait()
 
     def target_of(tt):
         gg = lax.shift_right_logical(tt, lK)
@@ -238,6 +240,17 @@
         stage_t[pl.ds(r, 2 * T, stride=8), :] = dot(pick, low)
     send_t[...] = stage_t[...].astype(BF).reshape(G, K, 16, W)
 
+    pl.semaphore_wait(barrier, (M * G - 1) + (Z - 1))
+
+    local(send_t.at[g], mid_t.at[g], 0)
+    group = [(dp, gg) for (dp, gg, _), (_, _, k) in zip(near, steps) if k == 0]
+    for dp, gg in group:
+        remote(send_t.at[gg], mid_t.at[g], 0, dp, m)
+    sent(mid_t.at[pl.ds(0, G - 1)], 0)
+    ins["mid_t"] = lambda: wait_in(mid_t, 0)
+
+    for i in (1, 2, 3, 4, 8):
+        loads[i].wait()
     bo = bown_ref[...]
     bo_row = bo.astype(F32)
     bo_col = to_col(bo_row, B3, iota((B3, B3), 0) == iota((B3, B3), 1))
@@ -269,38 +282,32 @@
     for t in range(T):
         send_r[t // K, t % K] = rows[t : t + 1, :]
 
-    pl.semaphore_wait(barrier, (M * G - 1) + (Z - 1))
-
     local(send_r.at[g], mid_r.at[g], 0, True)
-    local(send_t.at[g], mid_t.at[g], 0)
-
-    def fwd_a(t):
-        gg = lax.rem(g + t, G)
-        remote(send_r.at[gg], mid_r.at[g], 0, dp_of(gg, z), m, True)
-        remote(send_t.at[gg], mid_t.at[g], 0, dp_of(gg, z), m)
-
-    each(1, G, fwd_a)
+    for dp, gg in group:
+        remote(send_r.at[gg], mid_r.at[g], 0, dp, m, True)
     sent(mid_r.at[pl.ds(0, G - 1)], 0, True)
-    sent(mid_t.at[pl.ds(0, G - 1)], 0)
-    ins["mid"] = lambda: (wait_in(mid_r, 0, True), wait_in(mid_t, 0))
-    take("mid")
+    ins["mid_r"] = lambda: wait_in(mid_r, 0, True)
+
+    def fwd_b(mid, recv, small):
+        def to(k):
+            zz = base_z + M * k
+
+            @pl.when(zz != z)
+            def _():
+                remote(mid(k), recv.at[z], 1, dp_of(g, zz), m, small)
+
+            @pl.when(zz == z)
+            def _():
+                local(mid(k), recv.at[z], 1, small)
+
+        each(0, K, to)
+
+    take("mid_t")
+    fwd_b(lambda k: mid_t.at[:, k], recv_t, False)
+    take("mid_r")
     for t in range(T):
         mid_q[t % K, pl.ds(t // K, 1), :] = mid_r[t // K, t % K]
-
-    def fwd_b(k):
-        zz = base_z + M * k
-
-        @pl.when(zz != z)
-        def _():
-            remote(mid_q.at[k], recv_r.at[z], 1, dp_of(g, zz), m, True)
-            remote(mid_t.at[:, k], recv_t.at[z], 1, dp_of(g, zz), m)
-
-        @pl.when(zz == z)
-        def _():
-            local(mid_q.at[k], recv_r.at[z], 1, True)
-            local(mid_t.at[:, k], recv_t.at[z], 1)
-
-    each(0, K, fwd_b)
+    fwd_b(lambda k: mid_q.at[k], recv_r, True)
 
     def fwd_b_sent(n):
         if n:
@@ -414,8 +421,8 @@
     ins["slots"] = lambda: wait_in(slots, 4)
     take("slots")
 
-    for load in loads[9:]:
-        load.wait()
+    for i in (5, 6, 9, 10, 11):
+        loads[i].wait()
     table_s = slots[...].reshape(NS, W)
     feat[0] = dense_ref[...]
     for f in range(3):
@@ -433,6 +440,10 @@
     each(1, M, lambda t: remote(lbuf.at[m], lbuf.at[m], 3, me, lax.rem(m + t, M), True))
     sent(lbuf.at[pl.ds(0, M - 1)], 3, True)
     ins["logits"] = lambda: wait_in(lbuf.at[pl.ds(0, M - 1)], 3, True)
+    eye_w = onehot(iota((W, W), 0) == iota((W, W), 1))
+    for i in range(4):
+        turned = dot(eye_w, feat[i], ((1,), (1,))).astype(BF)
+        feat_t[i // 2, pl.ds((i % 2) * W, W), :] = turned
     take("logits")
 
     total = lbuf[0]
@@ -446,26 +457,13 @@
     other = 1 - c
     mate = me + 1 - 2 * c
 
-    def term_of(i, blk):
-        return dot(feat[i], blk, ((0,), (0,)))
-
     for q in range(S.Q):
-        low_q = grad_low[:, q * S.HQ : (q + 1) * S.HQ]
-        for h in range(C):
-
-            @pl.when(c != h)
-            def _():
-                for i in range(2):
-                    send_c[q, pl.ds(i * W, W), :] = term_of(2 * h + i, low_q).astype(BF)
-
-            @pl.when(c == h)
-            def _():
-                for i in range(2):
-                    keep_c[q, pl.ds(i * W, W), :] = term_of(2 * h + i, low_q)
-
+        send_c[q] = dot(feat_t[other], grad_low[:, q * S.HQ : (q + 1) * S.HQ]).astype(BF)
         remote(send_c.at[q], recv_c.at[q], 16 + q, mate, m)
         sent(send_c.at[q], 16 + q)
         ins["core", q] = lambda q=q: wait_in(recv_c.at[q], 16 + q)
+    for q in range(S.Q):
+        keep_c[q] = dot(feat_t[c], grad_low[:, q * S.HQ : (q + 1) * S.HQ])
 
     for f in range(3):
         term = dot(grad_low, w_ref[pl.ds((f + 1) * W, W), :], ((1,), (1,)))
@@ -679,6 +677,15 @@
     take("grads_x")
     each(0, Z // 2, update)
 
+    writes = []
+
+    def write(src, dst, i):
+        writes.append(pltpu.make_async_copy(src, dst, out_sem.at[i]))
+        writes[-1].start()
+
+    write(out_t, results[0], 0)
+    write(out_d, results[1], 1)
+
     def gather_core(q):
         take(("out_y", q))
         part = out_w.at[pl.ds(pl.multiple_of(c * hrows, 16), hrows), pl.ds(q * S.HQ, S.HQ)]
@@ -692,11 +699,19 @@
     remote(out_v.at[c], out_v.at[c], 15, mate, m, True)
     sent(vec_c, 15, True)
     ins["out_cv"] = lambda: wait_in(vec_c, 15, True)
+    own = pl.ds(pl.multiple_of(c * hrows, 16), hrows)
+    write(out_w.at[own], results[3].at[own], 3)
     out_s[...] = jnp.transpose(stage_s[...])[0:8, :]
+    write(out_s, results[2], 2)
     take("out_cv")
     for q in range(S.Q):
         take(("out_c", q))
+    far = pl.ds(pl.multiple_of(other * hrows, 16), hrows)
+    write(out_w.at[far], results[3].at[far], 4)
+    write(out_v, results[4], 5)
     assert not ins
+    for copy in writes:
+        copy.wait()
 
     for done in outs:
         done()
@@ -723,7 +738,6 @@
     C, Y, Z, M, K, G, N = S.C, S.Y, S.Z, S.M, S.K, S.G, S.N
     R2 = K * G * 8
     V = pltpu.VMEM
-    vmem = pl.BlockSpec(memory_space=pltpu.VMEM)
     hrows = 512 // C
     args = (
         new_owner.reshape(1, blocks),
@@ -739,17 +753,18 @@
         b_first.reshape(1, hidden),
         w_out.reshape(1, hidden),
     )
+    made = (
+        jax.ShapeDtypeStruct((blocks * 8, W), BF),
+        jax.ShapeDtypeStruct((blocks * 8, W), BF),
+        jax.ShapeDtypeStruct((8, blocks), F32),
+        jax.ShapeDtypeStruct((512, hidden), BF),
+        jax.ShapeDtypeStruct((C, Y, S.V, W), F32),
+    )
     out_t, out_d, out_s, out_w, out_v = pl.pallas_call(
         functools.partial(kernel, S),
-        out_shape=(
-            jax.ShapeDtypeStruct((blocks * 8, W), BF),
-            jax.ShapeDtypeStruct((blocks * 8, W), BF),
-            jax.ShapeDtypeStruct((8, blocks), F32),
-            jax.ShapeDtypeStruct((512, hidden), BF),
-            jax.ShapeDtypeStruct((C, Y, S.V, W), F32),
-        ),
+        out_shape=made,
         in_specs=[pl.BlockSpec(memory_space=pltpu.HBM)] * 12,
-        out_specs=(vmem,) * 5,
+        out_specs=(pl.BlockSpec(memory_space=pl.ANY),) * 5,
         scratch_shapes=[
             V((blocks, W), F32),
             V((2 * S.T * 8, W), F32),
@@ -768,6 +783,7 @@
             V((samples, hidden), F32),
             V((samples, hidden), F32),
             V((4, samples, W), BF),
+            V((C, 2 * W, samples), BF),
             V((3, samples, S.N * 8), BF),
             V((M, R2, 3 * samples), BF),
             V((2, R2, R2), BF),
@@ -794,15 +810,16 @@
             pltpu.SemaphoreType.DMA((32,)),
             pltpu.SemaphoreType.DMA((32,)),
             pltpu.SemaphoreType.DMA((12,)),
+            pltpu.SemaphoreType.DMA((6,)),
         ]
-        + [V(a.shape, a.dtype) for a in args],
+        + [V(a.shape, a.dtype) for a in args + made],
         compiler_params=pltpu.CompilerParams(
             collective_id=0, has_side_effects=True, vmem_limit_bytes=56 * 1024 * 1024
         ),
     )(*args)
     vecs = out_v.reshape(C, hidden)
     return (
-        (out_t.astype(F32) - out_d.astype(F32)).reshape(blocks, 8, W),
+        lax.optimization_barrier(out_t.astype(F32) - out_d.astype(F32)).reshape(blocks, 8, W),
         out_s.T,
         out_w,
         vecs[0],

time: 99.7 us -> 97.2 us (0.975); the launches traced: 98 us -> 96.9 us
  Pallas kernels: 92.7 us -> 91.6 us
    sub x0 -> x1, other arithmetic: none -> 2.36 us  [local_step(): out_t.astype(F32) - out_d.astype(F32)]
    reshape x1 -> x0, other arithmetic: 2.36 us -> none  [local_step(): (out_t.astype(F32) - out_d.astype(F32)).reshape(blocks, 8, W)]
    pallas_call x1, Pallas kernels: 92.7 us -> 91.6 us  [local_step(): pl.pallas_call(functools.partial(kernel, S), out_shape=made, in_specs=[pl...]
where the time goes in v3:
time: 97.2 us; the launch traced here: 96.9 us
  Pallas kernels  91.6 us (94%)
  other arithmetic  2.36 us (2%)
  local copies, waits for them, and re-layouts  2.28 us (2%)
    pallas_call x1, Pallas kernels, local_step(): pl.pallas_call(functools.partial(kernel, S), out_shape=made, in_specs=[pl...  91.6 us
    sub x1, other arithmetic, local_step(): out_t.astype(F32) - out_d.astype(F32)  2.36 us

profile of v3, /device:TPU:1, one launch (start us, length us, event | category | flops | bytes accessed | tf_op | source)
XLA Modules:
  0.0 96.9 jit_solution(12949368794617906608)
XLA Ops:
  0.6 91.6 %shard_map.155 = (bf16[2048,128]{1,0:T(8,128)(2,1)}, bf16[2048,128]{1,0:T(8,128)(2,1)}, f32[8,256]{1,0:T(8,128)}, bf16[512,1024]{1,0:T(8,128)(2,1)}, f32[2,4,2,128]{3,2,1,0:T(2,128)}) custom-call(s32[1,256]{1,0:T(1,128)} %bitcast.22, s32[1,384]{1,0:T(1,128)} %bitcast.21, s32[384]{0:T(512)} %refs_2_.1, s32[16,384]{1,0:T(8,128)} %bitcast.14, s32[384]{0:T(512)} %refs_4_.1, ...), custom_call_target="tpu_custom_call" | custom-call | tf_op jit(solution)/shard_map/pallas_call | solution.py:763
  92.3 0.0 copy-start.2
  92.3 0.0 copy-start
  92.3 2.4 %convert_subtract_fusion = f32[2048,128]{1,0:T(8,128)} fusion(bf16[2048,128]{1,0:T(8,128)(2,1)} %get-tuple-element.11, bf16[2048,128]{1,0:T(8,128)(2,1)} %get-tuple-element.10), kind=kLoop, calls=%fused_computation | loop fusion | flops 786432 | bytes 2097152 | tf_op jit(solution)/shard_map/sub | solution.py:822
  94.7 0.0 copy-done.2
  94.7 0.0 copy-start.1
  94.7 0.6 fusion
  95.3 0.1 copy-done.1
  95.4 0.6 copy.19
  96.0 0.0 copy-done
  96.0 1.0 %copy.20 = bf16[512,1024]{1,0:T(8,128)(2,1)} copy(bf16[512,1024]{1,0:T(8,128)(2,1)S(1)} %copy-done) | data formatting | bytes 2097152
Async XLA Ops:
  92.3 2.4 %copy-start.2 = (f32[2,4,2,128]{3,2,1,0:T(2,128)S(1)}, f32[2,4,2,128]{3,2,1,0:T(2,128)}, u32[]{:S(2)}) copy-start(f32[2,4,2,128]{3,2,1,0:T(2,128)} %get-tuple-element.14) | copy-start | bytes 24580
  92.3 3.7 %copy-start = (bf16[512,1024]{1,0:T(8,128)(2,1)S(1)}, bf16[512,1024]{1,0:T(8,128)(2,1)}, u32[]{:S(2)}) copy-start(bf16[512,1024]{1,0:T(8,128)(2,1)} %get-tuple-element.24) | copy-start | bytes 3145732
  94.7 0.7 copy-start.1

commit v4 on v3

--- a/solution.py
+++ b/solution.py
@@ -69,8 +69,8 @@
     S,
     *refs,
 ):
-    given, results, rest = refs[:12], refs[12:17], refs[17:]
-    held, made, inner = rest[-17:-5], rest[-5:], rest[:-17]
+    given, results, rest = refs[:12], refs[12:16], refs[16:]
+    held, made, inner = rest[-16:-4], rest[-4:], rest[:-16]
     run(S, given, held, results, *made, *inner)
 
 
@@ -80,7 +80,6 @@
     held,
     results,
     out_t,
-    out_d,
     out_s,
     out_w,
     out_v,
@@ -651,14 +650,13 @@
         pick_s = iota((QR, W), 1) == (iota((QR, W), 0) & 15) + 96
         st = jnp.sum(jnp.where(pick_s, wide_s, 0.0), axis=1, keepdims=True)
         st = st + jnp.sum(grad * grad, axis=1, keepdims=True) * (1.0 / W)
-        low = recv_t[i].reshape(QR, W)
-        step = (learn_rate * grad / (jnp.sqrt(st) + epsilon)).astype(BF)
+        low = recv_t[i].reshape(QR, W).astype(F32)
+        new = low - learn_rate * grad / (jnp.sqrt(st) + epsilon)
         pick_o = iota((QR, W), 1) == (iota((QR, W), 0) & 7)
         st8 = jnp.sum(jnp.where(pick_o, st, 0.0).reshape(QR // 8, 8, W), axis=1)
         for q in range(Y):
             at = pl.ds(pl.multiple_of((q * Z + i) * 32, 32), 32)
-            out_t[at, :] = low[q * 32 : (q + 1) * 32]
-            out_d[at, :] = step[q * 32 : (q + 1) * 32]
+            out_t[at, :] = new[q * 32 : (q + 1) * 32]
             stage_s[pl.ds((q * Z + i) * 4, 4), :] = st8[q * 4 : (q + 1) * 4]
 
     for q in range(S.Q):
@@ -684,7 +682,6 @@
         writes[-1].start()
 
     write(out_t, results[0], 0)
-    write(out_d, results[1], 1)
 
     def gather_core(q):
         take(("out_y", q))
@@ -700,15 +697,15 @@
     sent(vec_c, 15, True)
     ins["out_cv"] = lambda: wait_in(vec_c, 15, True)
     own = pl.ds(pl.multiple_of(c * hrows, 16), hrows)
-    write(out_w.at[own], results[3].at[own], 3)
+    write(out_w.at[own], results[2].at[own], 3)
     out_s[...] = jnp.transpose(stage_s[...])[0:8, :]
-    write(out_s, results[2], 2)
+    write(out_s, results[1], 2)
     take("out_cv")
     for q in range(S.Q):
         take(("out_c", q))
     far = pl.ds(pl.multiple_of(other * hrows, 16), hrows)
-    write(out_w.at[far], results[3].at[far], 4)
-    write(out_v, results[4], 5)
+    write(out_w.at[far], results[2].at[far], 4)
+    write(out_v, results[3], 5)
     assert not ins
     for copy in writes:
         copy.wait()
@@ -754,17 +751,16 @@
         w_out.reshape(1, hidden),
     )
     made = (
-        jax.ShapeDtypeStruct((blocks * 8, W), BF),
-        jax.ShapeDtypeStruct((blocks * 8, W), BF),
+        jax.ShapeDtypeStruct((blocks * 8, W), F32),
         jax.ShapeDtypeStruct((8, blocks), F32),
         jax.ShapeDtypeStruct((512, hidden), BF),
         jax.ShapeDtypeStruct((C, Y, S.V, W), F32),
     )
-    out_t, out_d, out_s, out_w, out_v = pl.pallas_call(
+    found = pl.pallas_call(
         functools.partial(kernel, S),
         out_shape=made,
         in_specs=[pl.BlockSpec(memory_space=pltpu.HBM)] * 12,
-        out_specs=(pl.BlockSpec(memory_space=pl.ANY),) * 5,
+        out_specs=(pl.BlockSpec(memory_space=pl.ANY),) * 4,
         scratch_shapes=[
             V((blocks, W), F32),
             V((2 * S.T * 8, W), F32),
@@ -817,14 +813,40 @@
             collective_id=0, has_side_effects=True, vmem_limit_bytes=56 * 1024 * 1024
         ),
     )(*args)
-    vecs = out_v.reshape(C, hidden)
+    part = jax.ShapeDtypeStruct((Y, S.V, W), F32)
+    out_t, out_s, out_w, b1, w2 = pl.pallas_call(
+        hand_over,
+        out_shape=(*made[:3], part, part),
+        in_specs=[pl.BlockSpec(memory_space=pl.ANY)] * 4,
+        out_specs=(pl.BlockSpec(memory_space=pl.ANY),) * 5,
+        scratch_shapes=[V(a.shape, a.dtype) for a in made]
+        + [pltpu.SemaphoreType.DMA((11,)), pltpu.SemaphoreType.DMA((11,))],
+    )(*found)
     return (
-        lax.optimization_barrier(out_t.astype(F32) - out_d.astype(F32)).reshape(blocks, 8, W),
+        out_t.reshape(blocks, 8, W),
         out_s.T,
         out_w,
-        vecs[0],
-        vecs[1],
+        b1.reshape(hidden),
+        w2.reshape(hidden),
     )
+
+
+def hand_over(t, s, w, v, out_t, out_s, out_w, out_b, out_u, vm_t, vm_s, vm_w, vm_v, sem_in, sem_out):
+    trips = []
+    for a, x, b in ((t, vm_t, out_t), (w, vm_w, out_w)):
+        n = a.shape[0] // 4
+        cuts = [pl.ds(i * n, n) for i in range(4)]
+        trips += [(a.at[p], x.at[p], b.at[p]) for p in cuts]
+    trips += [(s, vm_s, out_s), (v.at[0], vm_v.at[0], out_b), (v.at[1], vm_v.at[1], out_u)]
+    come = [pltpu.make_async_copy(a, x, sem_in.at[i]) for i, (a, x, _) in enumerate(trips)]
+    go = [pltpu.make_async_copy(x, b, sem_out.at[i]) for i, (_, x, b) in enumerate(trips)]
+    for copy in come:
+        copy.start()
+    for first, then in zip(come, go):
+        first.wait()
+        then.start()
+    for copy in go:
+        copy.wait()
 
 
 def solution(mesh):

time: 97.2 us -> 95 us (0.977)
  Pallas kernels: 91.6 us -> 94.2 us
  other arithmetic: 2.36 us -> 0 us
  local copies, waits for them, and re-layouts: 2.28 us -> 0 us
    pallas_call x0 -> x1, Pallas kernels: none -> 2.46 us  [local_step(): pl.pallas_call(hand_over, out_shape=(*made[:3], part, part), in_specs=[pl...]
    sub x1 -> x0, other arithmetic: 2.36 us -> none  [local_step(): out_t.astype(F32) - out_d.astype(F32)]
    unnamed x8 -> x0, local copies, waits for them, and re-layouts: 1.68 us -> none
where the time goes in v4:
time: 95 us; the launch traced here: 94.8 us
  Pallas kernels  94.2 us (99%)
    pallas_call x1, Pallas kernels, local_step(): pl.pallas_call(functools.partial(kernel, S), out_shape=made, in_specs=[pl...  91.7 us
    pallas_call x1, Pallas kernels, local_step(): pl.pallas_call(hand_over, out_shape=(*made[:3], part, part), in_specs=[pl...  2.46 us

profile of v4, /device:TPU:1, one launch (start us, length us, event | category | flops | bytes accessed | tf_op | source)
XLA Modules:
  0.0 94.8 jit_solution(296697787966756267)
XLA Ops:
  0.6 91.7 %shard_map.155 = (f32[2048,128]{1,0:T(8,128)}, f32[8,256]{1,0:T(8,128)}, bf16[512,1024]{1,0:T(8,128)(2,1)}, f32[2,4,2,128]{3,2,1,0:T(2,128)}) custom-call(s32[1,256]{1,0:T(1,128)} %bitcast.18, s32[1,384]{1,0:T(1,128)} %bitcast.17, s32[384]{0:T(512)} %refs_2_.1, s32[16,384]{1,0:T(8,128)} %bitcast.13, s32[384]{0:T(512)} %refs_4_.1, bf16[128,128]{1,0:T(8,128)(2,1)} %refs_5_.1, ...), custom_call_target="tpu_custom_call" | custom-call | tf_op jit(solution)/shard_map/pallas_call | solution.py:759
  92.4 2.5 %shard_map.156 = (f32[2048,128]{1,0:T(8,128)}, f32[8,256]{1,0:T(8,128)}, bf16[512,1024]{1,0:T(8,128)(2,1)}, f32[4,2,128]{2,1,0:T(2,128)}, f32[4,2,128]{2,1,0:T(2,128)}) custom-call(f32[2048,128]{1,0:T(8,128)} %get-tuple-element.14.t, f32[8,256]{1,0:T(8,128)} %get-tuple-element.15.s, bf16[512,1024]{1,0:T(8,128)(2,1)} %get-tuple-element.16.w, ...), custom_call_target="tpu_custom_call" | custom-call | tf_op jit(solution)/shard_map/pallas_call | solution.py:817

commit v5 on v4

--- a/solution.py
+++ b/solution.py
@@ -206,14 +206,13 @@
         each(0, Z - 1, step)
 
     along_z(lambda zz: greet(dp_of(g, zz), m))
-    loads = [pltpu.make_async_copy(a, h, in_sem.at[i]) for i, (a, h) in enumerate(zip(given, held))]
+    loads = [pltpu.make_async_copy(a, h if i != 7 else h.at[pl.ds(0, NB * 8)], in_sem.at[i]) for i, (a, h) in enumerate(zip(given, held))]
     for load in loads:
         load.start()
     for dp, _, mm in near:
         greet(dp, mm)
 
-    for i in (0, 7):
-        loads[i].wait()
+    loads[0].wait()
 
     def target_of(tt):
         gg = lax.shift_right_logical(tt, lK)
@@ -234,10 +233,11 @@
     want = target_of(lax.shift_right_logical(rows2, 1)).astype(F32)
     pick_f = jnp.where((own_row == want) & (rank_row == (rows2 & 1).astype(F32)), 1.0, 0.0)
     pick = pick_f.astype(BF)
+    loads[7].wait()
     for r in range(8):
         low = table_ref[pl.ds(r, NB, stride=8), :].astype(BF)
         stage_t[pl.ds(r, 2 * T, stride=8), :] = dot(pick, low)
-    send_t[...] = stage_t[...].astype(BF).reshape(G, K, 16, W)
+    send_t[...] = stage_t[pl.ds(0, 2 * T * 8), :].astype(BF).reshape(G, K, 16, W)
 
     pl.semaphore_wait(barrier, (M * G - 1) + (Z - 1))
 
@@ -285,7 +285,7 @@
     for dp, gg in group:
         remote(send_r.at[gg], mid_r.at[g], 0, dp, m, True)
     sent(mid_r.at[pl.ds(0, G - 1)], 0, True)
-    ins["mid_r"] = lambda: wait_in(mid_r, 0, True)
+    ins["mid_r"] = lambda: wait_in(mid_r.at[pl.ds(0, G)], 0, True)
 
     def fwd_b(mid, recv, small):
         def to(k):
@@ -494,13 +494,13 @@
         for j in range(HL // W):
             vec[i, j // S.V, pl.ds(j % S.V, 1), :] = row[:, j * W : (j + 1) * W]
 
-    remote(vec.at[other], vec_c, 6, mate, m, True)
-    sent(vec_c, 6, True)
-    ins["core_v"] = lambda: wait_in(vec_c, 6, True)
+    remote(vec.at[other], vec_c.at[pl.ds(0, Y)], 6, mate, m, True)
+    sent(vec_c.at[pl.ds(0, Y)], 6, True)
+    ins["core_v"] = lambda: wait_in(vec_c.at[pl.ds(0, Y)], 6, True)
 
 
     take("core_v")
-    vec[c] = vec[c] + vec_c[...]
+    vec[c] = vec[c] + vec_c[pl.ds(0, Y)]
 
     def to_y_vec(t):
         yy = lax.rem(y + t, Y)
@@ -562,11 +562,11 @@
     accv = vec[c, y]
     for t in range(1, Y):
         accv = accv + vec_y[lax.rem(y + t, Y)]
-    vec_ys[...] = accv
-    local(vec_ys, vec_z.at[z], 10, True)
-    along_z(lambda zz: remote(vec_ys, vec_z.at[z], 10, dp_of(g, zz), m, True))
+    vec_ys[0] = accv
+    local(vec_ys.at[0], vec_z.at[z], 10, True)
+    along_z(lambda zz: remote(vec_ys.at[0], vec_z.at[z], 10, dp_of(g, zz), m, True))
     sent(vec_z.at[pl.ds(0, Z - 1)], 10, True)
-    ins["dense_zv"] = lambda: wait_in(vec_z, 10, True)
+    ins["dense_zv"] = lambda: wait_in(vec_z.at[pl.ds(0, Z)], 10, True)
     def cast_t():
         for h in range(2):
             part = recv_t.at[pl.ds(h * (Z // 2), Z // 2)]
@@ -586,10 +586,10 @@
     def gather_z(q):
         take(("dense_z", q))
 
-        def add_z(i, carry):
-            return carry + recv_z[q, i].astype(F32)
-
-        acc = lax.fori_loop(0, Z, add_z, jnp.zeros((S.pr, S.pc), F32))
+        sums = [recv_z[q, i].astype(F32) for i in range(Z)]
+        while len(sums) > 1:
+            sums = [a + b for a, b in zip(sums[0::2], sums[1::2])]
+        acc = sums[0]
         r0 = pl.multiple_of(block0 + (z // S.CG) * S.pr, 16)
         c0 = pl.multiple_of(q * S.HQ + lax.rem(z, S.CG) * S.pc, W)
         out_w[pl.ds(r0, S.pr), pl.ds(c0, S.pc)] = acc.astype(BF)
@@ -694,18 +694,18 @@
         gather_core(q)
     take("out_yv")
     remote(out_v.at[c], out_v.at[c], 15, mate, m, True)
-    sent(vec_c, 15, True)
-    ins["out_cv"] = lambda: wait_in(vec_c, 15, True)
+    sent(vec_c.at[pl.ds(0, Y)], 15, True)
+    ins["out_cv"] = lambda: wait_in(vec_c.at[pl.ds(0, Y)], 15, True)
     own = pl.ds(pl.multiple_of(c * hrows, 16), hrows)
     write(out_w.at[own], results[2].at[own], 3)
-    out_s[...] = jnp.transpose(stage_s[...])[0:8, :]
+    out_s[...] = jnp.transpose(stage_s[pl.ds(0, NB), :])[0:8, :]
     write(out_s, results[1], 2)
     take("out_cv")
     for q in range(S.Q):
         take(("out_c", q))
     far = pl.ds(pl.multiple_of(other * hrows, 16), hrows)
     write(out_w.at[far], results[2].at[far], 4)
-    write(out_v, results[3], 5)
+    write(out_v.at[pl.ds(0, C)], results[3], 5)
     assert not ins
     for copy in writes:
         copy.wait()
@@ -762,13 +762,13 @@
         in_specs=[pl.BlockSpec(memory_space=pltpu.HBM)] * 12,
         out_specs=(pl.BlockSpec(memory_space=pl.ANY),) * 4,
         scratch_shapes=[
-            V((blocks, W), F32),
-            V((2 * S.T * 8, W), F32),
+            V((blocks + 8, W), F32),
+            V((2 * S.T * 8 + 8, W), F32),
             V((G, K, 16, W), BF),
-            V((G, K, 1, W), F32),
+            V((G + 8, K, 1, W), F32),
             V((G, K, 16, W), BF),
-            V((G, K, 1, W), F32),
-            V((K, G, W), F32),
+            V((G + 8, K, 1, W), F32),
+            V((K + 1, G, W), F32),
             V((Z, G, 16, W), BF),
             V((Z, G, W), F32),
             V((Z, G * 8, W), BF),
@@ -796,11 +796,11 @@
             V((S.Q, Y, S.RY, S.HQ), BF),
             V((S.Q, Z, S.pr, S.pc), BF),
             V((S.Q, Z, S.pr, S.pc), BF),
-            V((C, Y, S.V, W), F32),
-            V((Y, S.V, W), F32),
-            V((Y, S.V, W), F32),
-            V((S.V, W), F32),
-            V((Z, S.V, W), F32),
+            V((C + 2, Y, S.V, W), F32),
+            V((Y + 8, S.V, W), F32),
+            V((Y + 8, S.V, W), F32),
+            V((8, S.V, W), F32),
+            V((Z + 8, S.V, W), F32),
             pltpu.SemaphoreType.DMA((32,)),
             pltpu.SemaphoreType.DMA((32,)),
             pltpu.SemaphoreType.DMA((32,)),
@@ -808,7 +808,9 @@
             pltpu.SemaphoreType.DMA((12,)),
             pltpu.SemaphoreType.DMA((6,)),
         ]
-        + [V(a.shape, a.dtype) for a in args + made],
+        + [V((a.shape[0] + 8, W) if a.shape == (blocks * 8, W) else a.shape, a.dtype) for a in args]
+        + [V(a.shape, a.dtype) for a in made[:3]]
+        + [V((C + 2, Y, S.V, W), F32)],
         compiler_params=pltpu.CompilerParams(
             collective_id=0, has_side_effects=True, vmem_limit_bytes=56 * 1024 * 1024
         ),

time: 95 us -> 95 us (level)
  no operation moved by 1% of the time
where the time goes in v5:
time: 95 us; the launch traced here: 94.8 us
  Pallas kernels  94.2 us (99%)
    pallas_call x1, Pallas kernels, local_step(): pl.pallas_call(functools.partial(kernel, S), out_shape=made, in_specs=[pl...  91.7 us
    pallas_call x1, Pallas kernels, local_step(): pl.pallas_call(hand_over, out_shape=(*made[:3], part, part), in_specs=[pl...  2.46 us

profile of v5, /device:TPU:1, one launch (start us, length us, event | category | flops | bytes accessed | tf_op | source)
XLA Modules:
  0.0 94.8 jit_solution(5781249862159019802)
XLA Ops:
  0.6 91.7 %shard_map.155 = (f32[2048,128]{1,0:T(8,128)}, f32[8,256]{1,0:T(8,128)}, bf16[512,1024]{1,0:T(8,128)(2,1)}, f32[2,4,2,128]{3,2,1,0:T(2,128)}) custom-call(s32[1,256]{1,0:T(1,128)} %bitcast.18, s32[1,384]{1,0:T(1,128)} %bitcast.17, s32[384]{0:T(512)} %refs_2_.1, s32[16,384]{1,0:T(8,128)} %bitcast.13, s32[384]{0:T(512)} %refs_4_.1, bf16[128,128]{1,0:T(8,128)(2,1)} %refs_5_.1, ...), custom_call_target="tpu_custom_call" | custom-call | tf_op jit(solution)/shard_map/pallas_call | solution.py:759
  92.4 2.5 %shard_map.156 = (f32[2048,128]{1,0:T(8,128)}, f32[8,256]{1,0:T(8,128)}, bf16[512,1024]{1,0:T(8,128)(2,1)}, f32[4,2,128]{2,1,0:T(2,128)}, f32[4,2,128]{2,1,0:T(2,128)}) custom-call(f32[2048,128]{1,0:T(8,128)} %get-tuple-element.14.t, f32[8,256]{1,0:T(8,128)} %get-tuple-element.15.s, bf16[512,1024]{1,0:T(8,128)(2,1)} %get-tuple-element.16.w, ...), custom_call_target="tpu_custom_call" | custom-call | tf_op jit(solution)/shard_map/pallas_call | solution.py:819
